TPU v7x, 32 devices: a whole 2x2x4 slice. The times are simulated.
32 devices in a mesh: section: 4 (over y, x), dp: 8 (over z, core).
Axes of the slice: x: 2, y: 2, z: 4, core: 2. Of those that a mesh axis runs over, the one named last changes fastest.
Arguments:
- tokens: bfloat16 [1024, 8192], P('dp'), may hold values from -6 to 6
- cotangent: bfloat16 [1024, 8192], P('dp'), may hold values from -6 to 6
- gains: float32 [4, 8192], P('section'), may hold values from 0.5 to 1.5
- value_projection_weight: bfloat16 [4, 8192, 1024], P('section', 'dp'), may hold values from -0.0625 to 0.0625
- output_projection_weight: bfloat16 [4, 8192, 1024], P('section', 'dp'), may hold values from -0.1875 to 0.1875
- block_adapter_ids: int32 [8], replicated, may hold values from 0 to 63
- job_adapter: int32 [8, 64], replicated, may hold values from -1 to 63, as said below
- job_slab: int32 [8, 64], replicated, may hold values from -1 to 3, as said below
- token_counts: int32 [64], replicated, may hold values from 128 to 1023
- slot_adapter_params: bfloat16 [4, 512, 36864], P('section', 'dp'), may hold values from -0.29882812 to 0.29882812
- first_moment: float32 [4, 512, 36864], P('section', 'dp'), may hold values from -6 to 6
- second_moment: float32 [4, 512, 36864], P('section', 'dp'), may hold values from 0.1 to 10
Outputs:
- new_params: bfloat16 [4, 512, 36864], P('section', 'dp')
- new_first: float32 [4, 512, 36864], P('section', 'dp')
- new_second: float32 [4, 512, 36864], P('section', 'dp')
- user_panels: bfloat16 [4, 8, 147456], P('section', 'dp')
Inputs may be any that keep to these rules, and one draw needn't show every extreme that they name: `job_adapter`: row o lists the adapters of which owner o holds a slab, each once, followed by -1; the 4 slabs of every adapter are held by 4 different owners, and every slab of every adapter is held exactly once. `job_slab`: the slab held in the same entry of job_adapter; -1 exactly where job_adapter is -1.
All inputs are finite; a program needn't handle non-finite values.
Results may differ from a plain program's by a relative error of at most 0.001.
Values may be sent and summed in bfloat16 or wider, within the bound.
A program may use at most 128 MiB of HBM per device.

v0:
```python
import jax
import jax.numpy as jnp
from jax import lax
from jax.sharding import PartitionSpec as P

ADAPTER_RANK = 16
MROWS = 16


ADAPTER_SCALE = 2.0
LEARN_RATE = 0.001
BETA_FIRST = 0.9
BETA_SECOND = 0.999
ADAM_EPS = 1e-08
FIRST_FIX = 1.0 - 0.9**50 * 0.9**50
SECOND_FIX = 1.0 - 0.999**50 * 0.999**50
NORM_EPS = 1e-05


def from_behind(shard, axis, by):
    length = lax.axis_size(axis)
    pairs = [(i, i + by) for i in range(length) if 0 <= i + by < length]
    return lax.ppermute(shard, axis, pairs)


def contract_trailing(left, right):
    return lax.dot_general(
        left, right, (((1,), (1,)), ((), ())), preferred_element_type=jnp.float32
    )


def contract_leading(left, right):
    return lax.dot_general(
        left, right, (((0,), (0,)), ((), ())), preferred_element_type=jnp.float32
    )


def norm_rows(hidden_state, gain_vector_row):
    hidden_wide = hidden_state.astype(jnp.float32)
    mean_square = jnp.mean(hidden_wide * hidden_wide, axis=-1, keepdims=True)
    norm_gain_scale = lax.rsqrt(mean_square + NORM_EPS)
    normalized_rows = (hidden_wide * norm_gain_scale * gain_vector_row).astype(jnp.bfloat16)
    return (hidden_wide, norm_gain_scale, normalized_rows)


def layer_ahead_pass(
    hidden_state, gain_vector_row, value_complete, output_complete, adapter_down, adapter_up
):
    hidden_wide, norm_gain_scale, normalized_rows = norm_rows(hidden_state, gain_vector_row)
    rank_projected = jnp.dot(
        normalized_rows, adapter_down, preferred_element_type=jnp.float32
    ).astype(jnp.bfloat16)
    value_block_rows = (
        jnp.dot(normalized_rows, value_complete, preferred_element_type=jnp.float32)
        + ADAPTER_SCALE * jnp.dot(rank_projected, adapter_up, preferred_element_type=jnp.float32)
    ).astype(jnp.bfloat16)
    output_block_rows = (hidden_wide + contract_trailing(value_block_rows, output_complete)).astype(
        jnp.bfloat16
    )
    return (output_block_rows, norm_gain_scale, normalized_rows, rank_projected)


def layer_reverse_pass(
    output_gradient,
    hidden_state,
    norm_gain_scale,
    normalized_rows,
    rank_projected,
    gain_vector_row,
    value_complete,
    output_complete,
    adapter_down,
    adapter_up,
):
    value_gradient = jnp.dot(
        output_gradient, output_complete, preferred_element_type=jnp.float32
    ).astype(jnp.bfloat16)
    low_rank_gradient = (ADAPTER_SCALE * contract_trailing(value_gradient, adapter_up)).astype(
        jnp.bfloat16
    )
    down_gradient = contract_leading(normalized_rows, low_rank_gradient)
    up_gradient = ADAPTER_SCALE * contract_leading(rank_projected, value_gradient)
    normed_gradient = (
        contract_trailing(value_gradient, value_complete)
        + contract_trailing(low_rank_gradient, adapter_down)
    ) * gain_vector_row
    hidden_wide = hidden_state.astype(jnp.float32)
    centred = jnp.mean(hidden_wide * normed_gradient, axis=-1, keepdims=True)
    grad_in = (
        output_gradient.astype(jnp.float32)
        + norm_gain_scale * normed_gradient
        - hidden_wide * norm_gain_scale**3 * centred
    )
    return (grad_in.astype(jnp.bfloat16), down_gradient, up_gradient)


def adam_update(params_old, first_old, second_old, slot_grad, live):
    first_step = BETA_FIRST * first_old + (1.0 - BETA_FIRST) * slot_grad
    second_step = BETA_SECOND * second_old + (1.0 - BETA_SECOND) * slot_grad * slot_grad
    step_size = first_step / FIRST_FIX / (jnp.sqrt(second_step / SECOND_FIX) + ADAM_EPS)
    params_step = (params_old.astype(jnp.float32) - LEARN_RATE * step_size).astype(jnp.bfloat16)
    return (
        jnp.where(live, params_step, params_old),
        jnp.where(live, first_step, first_old),
        jnp.where(live, second_step, second_old),
    )


def put_slot(saved_array, new_value, slot_number, is_valid):
    current = lax.dynamic_index_in_dim(saved_array, slot_number, 0, keepdims=False)
    return lax.dynamic_update_index_in_dim(
        saved_array, jnp.where(is_valid, new_value, current), slot_number, 0
    )


def select_slot(saved_array, slot_number):
    return lax.dynamic_index_in_dim(saved_array, slot_number, 0, keepdims=False)


def on_device(
    tokens,
    cotangent,
    gains,
    value_projection_weight,
    output_projection_weight,
    block_adapter_ids,
    job_adapter,
    job_slab,
    token_counts,
    slot_adapter_params,
    first_moment,
    second_moment,
):
    section_index = lax.axis_index("section")
    owner_index = lax.axis_index("dp")
    section_total = lax.axis_size("section")
    owner_total = lax.axis_size("dp")
    tok_dev, hidden_width = tokens.shape
    value_feature_width = value_projection_weight.shape[2]
    panel_width = slot_adapter_params.shape[2]
    slab_count = owner_total // 2
    block_total = block_adapter_ids.shape[0]
    local_blocks = block_total // owner_total
    block_rows = tok_dev // local_blocks
    adapter_total = token_counts.shape[0]
    divide_position = hidden_width * ADAPTER_RANK
    value_complete, output_complete = (
        lax.all_gather(value_projection_weight, "dp", axis=1, tiled=True),
        lax.all_gather(output_projection_weight, "dp", axis=1, tiled=True),
    )
    value_complete = value_complete[0]
    output_complete = output_complete[0]
    gain_vector_row = gains[0]
    my_jobs = lax.dynamic_index_in_dim(job_adapter, owner_index, 0, keepdims=False)
    my_blocks = lax.dynamic_slice_in_dim(
        block_adapter_ids, owner_index * local_blocks, local_blocks
    )
    slab_ids = jnp.arange(slab_count, dtype=jnp.int32)
    matching = (job_adapter[None, None] == my_blocks[:, None, None, None]) & (
        job_slab[None, None] == slab_ids[None, :, None, None]
    )
    owner_ids = jnp.arange(owner_total, dtype=jnp.int32)
    source_owner = jnp.sum(jnp.where(matching, owner_ids[None, None, :, None], 0), axis=(2, 3))
    own_select = (block_adapter_ids[:, None] == my_jobs[None, :]) & (my_jobs[None, :] >= 0)
    slot_rows = jnp.arange(local_blocks, dtype=jnp.int32)[:, None]

    def hand_out(owned):
        picked = jnp.dot(own_select.astype(jnp.bfloat16), owned, preferred_element_type=jnp.float32)
        return picked.astype(jnp.bfloat16).reshape(owner_total, local_blocks, panel_width)

    def assemble(arrived):
        gathered_slabs = arrived[source_owner, slot_rows]
        return gathered_slabs.reshape(local_blocks, slab_count * panel_width)

    gathered_panels = assemble(
        lax.all_to_all(
            hand_out(slot_adapter_params[0]), "dp", split_axis=0, concat_axis=0, tiled=True
        )
    )
    adapter_down_every = gathered_panels[:, :divide_position].reshape(
        local_blocks, hidden_width, ADAPTER_RANK
    )
    adapter_up_every = gathered_panels[:, divide_position:].reshape(
        local_blocks, ADAPTER_RANK, value_feature_width
    )
    micro_rows = 2 * MROWS
    micro_count = tok_dev // micro_rows
    per_block = block_rows // micro_rows
    step_count = section_total + micro_count - 1
    token_micro = tokens.reshape(micro_count, micro_rows, hidden_width)
    cot_micro = cotangent.reshape(micro_count, micro_rows, hidden_width)

    def forward_step(state_tuple, step_number):
        incoming, saved_in, saved_scale, saved_normed, saved_low = state_tuple
        micro_index = step_number - section_index
        is_valid = (micro_index >= 0) & (micro_index < micro_count)
        micro_slot = jnp.clip(micro_index, 0, micro_count - 1)
        hidden_state = jnp.where(section_index == 0, select_slot(token_micro, micro_slot), incoming)
        block_slot_index = micro_slot // per_block

        def forward_run_layer(unused):
            return layer_ahead_pass(
                hidden_state,
                gain_vector_row,
                value_complete,
                output_complete,
                select_slot(adapter_down_every, block_slot_index),
                select_slot(adapter_up_every, block_slot_index),
            )

        def forward_skip_layer(unused):
            return (
                jnp.zeros((micro_rows, hidden_width), jnp.bfloat16),
                jnp.zeros((micro_rows, 1), jnp.float32),
                jnp.zeros((micro_rows, hidden_width), jnp.bfloat16),
                jnp.zeros((micro_rows, ADAPTER_RANK), jnp.bfloat16),
            )

        output_block_rows, norm_gain_scale, normalized_rows, rank_projected = lax.cond(
            is_valid, forward_run_layer, forward_skip_layer, None
        )
        saved_in = put_slot(saved_in, hidden_state, micro_slot, is_valid)
        saved_scale = put_slot(saved_scale, norm_gain_scale, micro_slot, is_valid)
        saved_normed = put_slot(saved_normed, normalized_rows, micro_slot, is_valid)
        saved_low = put_slot(saved_low, rank_projected, micro_slot, is_valid)
        passed = from_behind(output_block_rows, "section", 1)
        return ((passed, saved_in, saved_scale, saved_normed, saved_low), None)

    forward_init = (
        jnp.zeros((micro_rows, hidden_width), jnp.bfloat16),
        jnp.zeros((micro_count, micro_rows, hidden_width), jnp.bfloat16),
        jnp.zeros((micro_count, micro_rows, 1), jnp.float32),
        jnp.zeros((micro_count, micro_rows, hidden_width), jnp.bfloat16),
        jnp.zeros((micro_count, micro_rows, ADAPTER_RANK), jnp.bfloat16),
    )
    forward_done, _ = lax.scan(forward_step, forward_init, jnp.arange(step_count, dtype=jnp.int32))
    _, saved_in, saved_scale, saved_normed, saved_low = forward_done

    def backward_step(state_tuple, step_number):
        incoming, block_grads = state_tuple
        micro_index = step_number - (section_total - 1 - section_index)
        is_valid = (micro_index >= 0) & (micro_index < micro_count)
        micro_slot = jnp.clip(micro_index, 0, micro_count - 1)
        output_gradient = jnp.where(
            section_index == section_total - 1, select_slot(cot_micro, micro_slot), incoming
        )
        block_slot_index = micro_slot // per_block

        def backward_run_layer(unused):
            return layer_reverse_pass(
                output_gradient,
                select_slot(saved_in, micro_slot),
                select_slot(saved_scale, micro_slot),
                select_slot(saved_normed, micro_slot),
                select_slot(saved_low, micro_slot),
                gain_vector_row,
                value_complete,
                output_complete,
                select_slot(adapter_down_every, block_slot_index),
                select_slot(adapter_up_every, block_slot_index),
            )

        def backward_skip_layer(unused):
            return (
                jnp.zeros((micro_rows, hidden_width), jnp.bfloat16),
                jnp.zeros((hidden_width, ADAPTER_RANK), jnp.float32),
                jnp.zeros((ADAPTER_RANK, value_feature_width), jnp.float32),
            )

        grad_in, down_gradient, up_gradient = lax.cond(
            is_valid, backward_run_layer, backward_skip_layer, None
        )
        grad_term = jnp.concatenate([down_gradient.reshape(-1), up_gradient.reshape(-1)])
        block_grads = block_grads.at[block_slot_index].add(jnp.where(is_valid, grad_term, 0.0))
        passed = from_behind(grad_in, "section", -1)
        return ((passed, block_grads), None)

    backward_init = (
        jnp.zeros((micro_rows, hidden_width), jnp.bfloat16),
        jnp.zeros((local_blocks, slab_count * panel_width), jnp.float32),
    )
    backward_done, _ = lax.scan(
        backward_step, backward_init, jnp.arange(step_count, dtype=jnp.int32)
    )
    block_grads = backward_done[1]
    outgoing = (
        jnp.zeros((owner_total, local_blocks, panel_width), jnp.float32)
        .at[source_owner, slot_rows]
        .set(block_grads.reshape(local_blocks, slab_count, panel_width))
    )
    arrived = lax.all_to_all(
        outgoing.astype(jnp.bfloat16), "dp", split_axis=0, concat_axis=0, tiled=True
    ).astype(outgoing.dtype)
    summed = jnp.dot(
        own_select.astype(jnp.float32).T,
        arrived.reshape(block_total, panel_width),
        precision=lax.Precision.HIGHEST,
        preferred_element_type=jnp.float32,
    )
    live = my_jobs >= 0
    adapter_ids = jnp.arange(adapter_total, dtype=jnp.int32)
    slot_counts = jnp.sum(
        jnp.where(adapter_ids[None, :] == my_jobs[:, None], token_counts[None, :], 0), axis=1
    )
    slot_counts = jnp.where(live, slot_counts, 1)
    slot_grad = summed / slot_counts.astype(jnp.float32)[:, None]
    params_new, first_new, second_new = adam_update(
        slot_adapter_params[0], first_moment[0], second_moment[0], slot_grad, live[:, None]
    )
    returned = assemble(
        lax.all_to_all(hand_out(params_new), "dp", split_axis=0, concat_axis=0, tiled=True)
    )
    return (params_new[None], first_new[None], second_new[None], returned[None])


def solution(mesh):
    return jax.shard_map(
        on_device,
        mesh=mesh,
        in_specs=(
            P("dp", None),
            P("dp", None),
            P("section", None),
            P("section", "dp", None),
            P("section", "dp", None),
            P(),
            P(),
            P(),
            P(),
            P("section", "dp", None),
            P("section", "dp", None),
            P("section", "dp", None),
        ),
        out_specs=(
            P("section", "dp", None),
            P("section", "dp", None),
            P("section", "dp", None),
            P("section", "dp", None),
        ),
        check_vma=False,
    )
```

profile of v0, /device:TPU:0, one launch (start us, length us, event | category | flops | bytes accessed | tf_op | source)
XLA Modules:
  0.0 992.9 jit_solution(8253172100476830092)
XLA Ops:
  16.5 6.3 all-to-all-start
  24.9 31.7 %all-to-all-done = bf16[8,2,18432]{2,1,0:T(2,128)(2,1)S(1)} async-done(((bf16[8,2,18432]{2,1,0:T(2,128)(2,1)}), bf16[8,2,18432]{2,1,0:T(2,128)(2,1)S(1)}, u32[]{:S(2)}, u32[]{:S(2)}) %all-to-all-start) | async-done | bytes 589856 | tf_op jit(solution)/shard_map/all_to_all | solution.py:176
  64.7 111.3 %all-gather.3.cloned.1.call-done = bf16[1,8192,1024]{2,1,0:T(8,128)(2,1)} async-done(((bf16[1,1024,1024]{2,1,0:T(8,128)(2,1)}), bf16[1,8192,1024]{2,1,0:T(8,128)(2,1)}) %all-gather.3.cloned.1.call-update) | async-done | bytes 16777232 | tf_op jit(solution)/shard_map/all_gather | solution.py:148
  176.0 150.9 %all-gather.5.cloned.1.call-done = bf16[1,8192,1024]{2,1,0:T(8,128)(2,1)} async-done(((bf16[1,1024,1024]{2,1,0:T(8,128)(2,1)}), bf16[1,8192,1024]{2,1,0:T(8,128)(2,1)}) %all-gather.5.cloned.1.call-update) | async-done | bytes 16777232 | tf_op jit(solution)/shard_map/all_gather | solution.py:149
  329.8 248.2 %while.36 = (s32[]{:T(128)}, bf16[32,8192]{1,0:T(8,128)(2,1)S(1)}, bf16[4,32,8192]{2,1,0:T(8,128)(2,1)S(1)}, f32[4,32,1]{1,2,0:T(1,128)}, bf16[4,32,8192]{2,1,0:...) while((s32[]{:T(128)}, bf16[32,8192]{1,0:T(8,128)(2,1)S(1)}, ...), condition=%wide.region_5.6_spmd, body=%wide.region_1.5_spmd.sunk | while | flops 1086686208 | bytes 48315820 | solution.py:236
  333.0 20.2 %conditional.5 = (bf16[32,8192]{1,0:T(8,128)(2,1)S(1)}, f32[32,1]{0,1:T(1,128)}, bf16[32,8192]{1,0:T(8,128)(2,1)}, bf16[32,16]{0,1:T(8,128)(2,1)}) conditional(s32[]{:T(128)} %convert_element_type.136, () %tuple.117, (bf16[32,8192]{1,0:T(8,128)(2,1)S(1)}, f32[1,8192]{1,0:T(1,128)}, bf16[8192,1024]{1,0:T(8,128)(2,1)}, ...), branch_computations={%region_2.2_spmd, %region_3.4_spmd} | conditional | flops 1085899264 | bytes 37816992 | solution.py:219
  338.4 14.8 %fusion = bf16[32,8192]{1,0:T(8,128)(2,1)S(1)} fusion(bf16[8192,1024]{1,0:T(8,128)(2,1)} %get-tuple-element.485, bf16[32,8192]{1,0:T(8,128)(2,1)S(1)} %get-tuple-element.480, f32[32,1024]{1,0:T(8,128)S(1)} %convolution_multiply_fusion, bf16[32,8192]{1,0:T(8,128)(2,1)} %fusion.4, bf16[8192,1024]{1,0:T(8,128)(2,1)} %get-tuple-element.482), kind=kOutput, calls=%fused_computation.4 | convolution fusion | flops 1074593792 | bytes 35258368 | tf_op jit(solution)/shard_map/while/body/eval_jaxpr/cond/branch_1_fun/dot_general | solution.py:27
  360.8 6.6 collective-permute-done
  370.6 20.2 %conditional.5 = (bf16[32,8192]{1,0:T(8,128)(2,1)S(1)}, f32[32,1]{0,1:T(1,128)}, bf16[32,8192]{1,0:T(8,128)(2,1)}, bf16[32,16]{0,1:T(8,128)(2,1)}) conditional(s32[]{:T(128)} %convert_element_type.136, () %tuple.117, (bf16[32,8192]{1,0:T(8,128)(2,1)S(1)}, f32[1,8192]{1,0:T(1,128)}, bf16[8192,1024]{1,0:T(8,128)(2,1)}, ...), branch_computations={%region_2.2_spmd, %region_3.4_spmd} | conditional | flops 1085899264 | bytes 37816992 | solution.py:219
  376.0 14.8 %fusion = bf16[32,8192]{1,0:T(8,128)(2,1)S(1)} fusion(bf16[8192,1024]{1,0:T(8,128)(2,1)} %get-tuple-element.485, bf16[32,8192]{1,0:T(8,128)(2,1)S(1)} %get-tuple-element.480, f32[32,1024]{1,0:T(8,128)S(1)} %convolution_multiply_fusion, bf16[32,8192]{1,0:T(8,128)(2,1)} %fusion.4, bf16[8192,1024]{1,0:T(8,128)(2,1)} %get-tuple-element.482), kind=kOutput, calls=%fused_computation.4 | convolution fusion | flops 1074593792 | bytes 35258368 | tf_op jit(solution)/shard_map/while/body/eval_jaxpr/cond/branch_1_fun/dot_general | solution.py:27
  401.5 5.8 collective-permute-done
  410.5 20.2 %conditional.5 = (bf16[32,8192]{1,0:T(8,128)(2,1)S(1)}, f32[32,1]{0,1:T(1,128)}, bf16[32,8192]{1,0:T(8,128)(2,1)}, bf16[32,16]{0,1:T(8,128)(2,1)}) conditional(s32[]{:T(128)} %convert_element_type.136, () %tuple.117, (bf16[32,8192]{1,0:T(8,128)(2,1)S(1)}, f32[1,8192]{1,0:T(1,128)}, bf16[8192,1024]{1,0:T(8,128)(2,1)}, ...), branch_computations={%region_2.2_spmd, %region_3.4_spmd} | conditional | flops 1085899264 | bytes 37816992 | solution.py:219
  415.9 14.8 %fusion = bf16[32,8192]{1,0:T(8,128)(2,1)S(1)} fusion(bf16[8192,1024]{1,0:T(8,128)(2,1)} %get-tuple-element.485, bf16[32,8192]{1,0:T(8,128)(2,1)S(1)} %get-tuple-element.480, f32[32,1024]{1,0:T(8,128)S(1)} %convolution_multiply_fusion, bf16[32,8192]{1,0:T(8,128)(2,1)} %fusion.4, bf16[8192,1024]{1,0:T(8,128)(2,1)} %get-tuple-element.482), kind=kOutput, calls=%fused_computation.4 | convolution fusion | flops 1074593792 | bytes 35258368 | tf_op jit(solution)/shard_map/while/body/eval_jaxpr/cond/branch_1_fun/dot_general | solution.py:27
  441.4 4.9 collective-permute-done
  449.5 20.2 %conditional.5 = (bf16[32,8192]{1,0:T(8,128)(2,1)S(1)}, f32[32,1]{0,1:T(1,128)}, bf16[32,8192]{1,0:T(8,128)(2,1)}, bf16[32,16]{0,1:T(8,128)(2,1)}) conditional(s32[]{:T(128)} %convert_element_type.136, () %tuple.117, (bf16[32,8192]{1,0:T(8,128)(2,1)S(1)}, f32[1,8192]{1,0:T(1,128)}, bf16[8192,1024]{1,0:T(8,128)(2,1)}, ...), branch_computations={%region_2.2_spmd, %region_3.4_spmd} | conditional | flops 1085899264 | bytes 37816992 | solution.py:219
  454.9 14.8 %fusion = bf16[32,8192]{1,0:T(8,128)(2,1)S(1)} fusion(bf16[8192,1024]{1,0:T(8,128)(2,1)} %get-tuple-element.485, bf16[32,8192]{1,0:T(8,128)(2,1)S(1)} %get-tuple-element.480, f32[32,1024]{1,0:T(8,128)S(1)} %convolution_multiply_fusion, bf16[32,8192]{1,0:T(8,128)(2,1)} %fusion.4, bf16[8192,1024]{1,0:T(8,128)(2,1)} %get-tuple-element.482), kind=kOutput, calls=%fused_computation.4 | convolution fusion | flops 1074593792 | bytes 35258368 | tf_op jit(solution)/shard_map/while/body/eval_jaxpr/cond/branch_1_fun/dot_general | solution.py:27
  490.4 22.9 %collective-permute-start = (bf16[32,8192]{1,0:T(8,128)(2,1)}, bf16[32,8192]{1,0:T(8,128)(2,1)S(1)}, u32[]{:S(2)}, u32[]{:S(2)}) collective-permute-start(bf16[32,8192]{1,0:T(8,128)(2,1)} %copy-done), channel_id=1, source_target_pairs={{0,8},{8,16},{16,24},{1,9},{9,17},{17,25},{2,10},{10,18},{18,26},{... | collective-permute-start | bytes 1572872 | tf_op jit(solution)/shard_map/while/body/eval_jaxpr/ppermute | solution.py:23
  516.4 5.8 collective-permute-done
  528.2 5.2 collective-permute-start
  536.6 4.9 collective-permute-done
  547.5 23.4 %collective-permute-start = (bf16[32,8192]{1,0:T(8,128)(2,1)}, bf16[32,8192]{1,0:T(8,128)(2,1)S(1)}, u32[]{:S(2)}, u32[]{:S(2)}) collective-permute-start(bf16[32,8192]{1,0:T(8,128)(2,1)} %copy-done), channel_id=1, source_target_pairs={{0,8},{8,16},{16,24},{1,9},{9,17},{17,25},{2,10},{10,18},{18,26},{... | collective-permute-start | bytes 1572872 | tf_op jit(solution)/shard_map/while/body/eval_jaxpr/ppermute | solution.py:23
  578.6 328.3 %while.37 = (s32[]{:T(128)}, bf16[32,8192]{1,0:T(8,128)(2,1)S(1)}, f32[1,147456]{1,0:T(1,128)}, s32[7]{0:T(128)}, s32[]{:T(128)}, /*index=5*/pred[]{:T(512)}, bf...) while((s32[]{:T(128)}, bf16[32,8192]{1,0:T(8,128)(2,1)S(1)}, ...), condition=%wide.region_11.12_spmd.clone, body=%wide.region_6.11_spmd.clone.sunk | while | flops 1097335936 | bytes 48441136 | solution.py:282
  587.5 6.9 collective-permute-done.1
  604.0 20.5 %collective-permute-done.1 = bf16[32,8192]{1,0:T(8,128)(2,1)S(1)} collective-permute-done((bf16[32,8192]{1,0:T(8,128)(2,1)}, bf16[32,8192]{1,0:T(8,128)(2,1)S(1)}, u32[]{:S(2)}, u32[]{:S(2)}) %collective-permute-start.1) | collective-permute-done | bytes 524320 | tf_op jit(solution)/shard_map/while/body/eval_jaxpr/ppermute | solution.py:23
  634.2 93.7 %collective-permute-done.1 = bf16[32,8192]{1,0:T(8,128)(2,1)S(1)} collective-permute-done((bf16[32,8192]{1,0:T(8,128)(2,1)}, bf16[32,8192]{1,0:T(8,128)(2,1)S(1)}, u32[]{:S(2)}, u32[]{:S(2)}) %collective-permute-start.1) | collective-permute-done | bytes 524320 | tf_op jit(solution)/shard_map/while/body/eval_jaxpr/ppermute | solution.py:23
  729.7 30.9 %conditional.6 = (bf16[32,8192]{1,0:T(8,128)(2,1)}, f32[1,131072]{1,0:T(1,128)S(1)}, f32[1,16384]{1,0:T(1,128)S(1)}) conditional(s32[]{:T(128)} %convert_element_type.137, () %tuple.120, (pred[]{:T(512)}, bf16[4,32,8192]{2,1,0:T(8,128)(2,1)}, s32[]{:T(128)}, bf16[32,8192]{1,0:T(8,128)(2,1)S(1)}, f32[4,32,1]{1,2,0:T(1,128)}, ...), branch_computations={%region_7.7_spmd, %region_8.9_spmd} | conditional | flops 1096598656 | bytes 44573964 | solution.py:270
  729.7 8.9 convolution_convert_fusion.1
  738.8 10.8 %fusion.54 = f32[32,8192]{1,0:T(8,128)S(1)} fusion(bf16[32,1024]{1,0:T(8,128)(2,1)S(1)} %convolution_convert_fusion.1, bf16[8192,1024]{1,0:T(8,128)(2,1)} %get-tuple-element.512), kind=kOutput, calls=%fused_computation.115 | convolution fusion | flops 536870912 | bytes 17891328 | tf_op jit(solution)/shard_map/while/body/eval_jaxpr/cond/branch_1_fun/dot_general | solution.py:27
  762.7 4.6 broadcast_select_fusion.5
  767.2 5.6 collective-permute-done.1
  774.7 30.9 %conditional.6 = (bf16[32,8192]{1,0:T(8,128)(2,1)}, f32[1,131072]{1,0:T(1,128)S(1)}, f32[1,16384]{1,0:T(1,128)S(1)}) conditional(s32[]{:T(128)} %convert_element_type.137, () %tuple.120, (pred[]{:T(512)}, bf16[4,32,8192]{2,1,0:T(8,128)(2,1)}, s32[]{:T(128)}, bf16[32,8192]{1,0:T(8,128)(2,1)S(1)}, f32[4,32,1]{1,2,0:T(1,128)}, ...), branch_computations={%region_7.7_spmd, %region_8.9_spmd} | conditional | flops 1096598656 | bytes 44573964 | solution.py:270
  774.7 8.9 convolution_convert_fusion.1
  783.8 10.8 %fusion.54 = f32[32,8192]{1,0:T(8,128)S(1)} fusion(bf16[32,1024]{1,0:T(8,128)(2,1)S(1)} %convolution_convert_fusion.1, bf16[8192,1024]{1,0:T(8,128)(2,1)} %get-tuple-element.512), kind=kOutput, calls=%fused_computation.115 | convolution fusion | flops 536870912 | bytes 17891328 | tf_op jit(solution)/shard_map/while/body/eval_jaxpr/cond/branch_1_fun/dot_general | solution.py:27
  807.7 4.6 broadcast_select_fusion.5
  812.2 5.6 collective-permute-done.1
  819.7 30.9 %conditional.6 = (bf16[32,8192]{1,0:T(8,128)(2,1)}, f32[1,131072]{1,0:T(1,128)S(1)}, f32[1,16384]{1,0:T(1,128)S(1)}) conditional(s32[]{:T(128)} %convert_element_type.137, () %tuple.120, (pred[]{:T(512)}, bf16[4,32,8192]{2,1,0:T(8,128)(2,1)}, s32[]{:T(128)}, bf16[32,8192]{1,0:T(8,128)(2,1)S(1)}, f32[4,32,1]{1,2,0:T(1,128)}, ...), branch_computations={%region_7.7_spmd, %region_8.9_spmd} | conditional | flops 1096598656 | bytes 44573964 | solution.py:270
  819.7 8.9 convolution_convert_fusion.1
  828.8 10.8 %fusion.54 = f32[32,8192]{1,0:T(8,128)S(1)} fusion(bf16[32,1024]{1,0:T(8,128)(2,1)S(1)} %convolution_convert_fusion.1, bf16[8192,1024]{1,0:T(8,128)(2,1)} %get-tuple-element.512), kind=kOutput, calls=%fused_computation.115 | convolution fusion | flops 536870912 | bytes 17891328 | tf_op jit(solution)/shard_map/while/body/eval_jaxpr/cond/branch_1_fun/dot_general | solution.py:27
  852.7 4.6 broadcast_select_fusion.5
  857.2 5.6 collective-permute-done.1
  864.6 30.9 %conditional.6 = (bf16[32,8192]{1,0:T(8,128)(2,1)}, f32[1,131072]{1,0:T(1,128)S(1)}, f32[1,16384]{1,0:T(1,128)S(1)}) conditional(s32[]{:T(128)} %convert_element_type.137, () %tuple.120, (pred[]{:T(512)}, bf16[4,32,8192]{2,1,0:T(8,128)(2,1)}, s32[]{:T(128)}, bf16[32,8192]{1,0:T(8,128)(2,1)S(1)}, f32[4,32,1]{1,2,0:T(1,128)}, ...), branch_computations={%region_7.7_spmd, %region_8.9_spmd} | conditional | flops 1096598656 | bytes 44573964 | solution.py:270
  864.7 8.9 convolution_convert_fusion.1
  873.8 10.8 %fusion.54 = f32[32,8192]{1,0:T(8,128)S(1)} fusion(bf16[32,1024]{1,0:T(8,128)(2,1)S(1)} %convolution_convert_fusion.1, bf16[8192,1024]{1,0:T(8,128)(2,1)} %get-tuple-element.512), kind=kOutput, calls=%fused_computation.115 | convolution fusion | flops 536870912 | bytes 17891328 | tf_op jit(solution)/shard_map/while/body/eval_jaxpr/cond/branch_1_fun/dot_general | solution.py:27
  902.2 4.7 collective-permute-done.1
  907.4 6.7 reduce.19
  923.2 15.1 %all-to-all-done.1 = bf16[8,2,18432]{2,1,0:T(2,128)(2,1)S(1)} async-done(((bf16[8,2,18432]{2,1,0:T(2,128)(2,1)}), bf16[8,2,18432]{2,1,0:T(2,128)(2,1)S(1)}, u32[]{:S(2)}, u32[]{:S(2)}) %all-to-all-start.1) | async-done | bytes 589856 | tf_op jit(solution)/shard_map/all_to_all | solution.py:291
  938.9 16.2 %fusion.34 = (bf16[64,36864]{1,0:T(8,128)(2,1)S(1)}, f32[64,36864]{1,0:T(8,128)}) fusion(f32[1,64,36864]{2,1,0:T(8,128)} %param.33, f32[1,64,36864]{2,1,0:T(8,128)} %param.32, bf16[1,64,36864]{2,1,0:T(8,128)(2,1)} %param.31, pred[64]{0:T(512)(128)(4,1)S(1)} %copy-done.14, f32[64]{0:T(128)S(1)} %select_convert_fusion, ...), kind=kOutput, calls=%fused_computation.80 | convolution fusion | flops 77857792 | bytes 38339232 | tf_op jit(solution)/shard_map/dot_general | solution.py:294
  964.2 17.6 %fusion.31 = (f32[1,64,36864]{2,1,0:T(8,128)}, f32[1,64,36864]{2,1,0:T(8,128)}) fusion(f32[1,64,36864]{2,1,0:T(8,128)} %param.33, f32[64,36864]{1,0:T(8,128)} %get-tuple-element.809, pred[64]{0:T(512)(128)(4,1)S(1)} %copy-done.14, f32[1,64,36864]{2,1,0:T(8,128)} %param.32), kind=kLoop, calls=%fused_computation.74 | loop fusion | flops 21233664 | bytes 47185984 | tf_op jit(solution)/shard_map/broadcast_in_dim | solution.py:313
  (280 shorter events, 247.9 us)
Async XLA Ops:
  7.2 16.3 %copy-start.6 = (s32[8,64]{1,0:T(8,128)S(1)}, s32[8,64]{1,0:T(8,128)}, u32[]{:S(2)}) copy-start(s32[8,64]{1,0:T(8,128)} %param.28) | copy-start | bytes 6148
  7.2 15.7 %copy-start.10 = (s32[8]{0:T(128)S(1)}, s32[8]{0:T(128)}, u32[]{:S(2)}) copy-start(s32[8]{0:T(128)} %param.27) | copy-start | bytes 100
  7.2 16.9 %copy-start.9 = (s32[8,64]{1,0:T(8,128)S(1)}, s32[8,64]{1,0:T(8,128)}, u32[]{:S(2)}) copy-start(s32[8,64]{1,0:T(8,128)} %param.29) | copy-start | bytes 6148
  7.2 168.8 %all-gather.3.cloned.1.call-start = ((), (), s32[]{:S(2)}) async-start(), calls=%async_computation.3 | async-start | bytes 18874368 | tf_op jit(solution)/shard_map/all_gather | solution.py:148
  7.9 319.0 %all-gather.5.cloned.1.call-start = ((), (), s32[]{:S(2)}) async-start(), calls=%async_computation.4 | async-start | bytes 18874368 | tf_op jit(solution)/shard_map/all_gather | solution.py:149
  9.4 4.4 copy-start.12
  10.6 3.1 copy-start.7
  16.5 40.1 %all-to-all-start = ((bf16[8,2,18432]{2,1,0:T(2,128)(2,1)}), bf16[8,2,18432]{2,1,0:T(2,128)(2,1)S(1)}, u32[]{:S(2)}, u32[]{:S(2)}) async-start(bf16[8,2,18432]{2,1,0:T(2,128)(2,1)} %reshape.276), calls=%async_computation | async-start | bytes 1179648 | tf_op jit(solution)/shard_map/all_to_all | solution.py:176
  24.9 35.3 %copy-start.4 = (s32[4]{0:T(128)}, s32[4]{0:T(128)S(1)}, u32[]{:S(2)}) copy-start(s32[4]{0:T(128)S(1)} %get-tuple-element.806) | copy-start | bytes 52
  353.2 0.8 copy-start
  354.0 13.5 %collective-permute-start = (bf16[32,8192]{1,0:T(8,128)(2,1)}, bf16[32,8192]{1,0:T(8,128)(2,1)S(1)}, u32[]{:S(2)}, u32[]{:S(2)}) collective-permute-start(bf16[32,8192]{1,0:T(8,128)(2,1)} %copy-done), channel_id=1, source_target_pairs={{0,8},{8,16},{16,24},{1,9},{9,17},{17,25},{2,10},{10,18},{18,26},{... | collective-permute-start | bytes 1572872 | tf_op jit(solution)/shard_map/while/body/eval_jaxpr/ppermute | solution.py:23
  390.9 0.8 copy-start
  391.7 15.7 %collective-permute-start = (bf16[32,8192]{1,0:T(8,128)(2,1)}, bf16[32,8192]{1,0:T(8,128)(2,1)S(1)}, u32[]{:S(2)}, u32[]{:S(2)}) collective-permute-start(bf16[32,8192]{1,0:T(8,128)(2,1)} %copy-done), channel_id=1, source_target_pairs={{0,8},{8,16},{16,24},{1,9},{9,17},{17,25},{2,10},{10,18},{18,26},{... | collective-permute-start | bytes 1572872 | tf_op jit(solution)/shard_map/while/body/eval_jaxpr/ppermute | solution.py:23
  430.7 0.8 copy-start
  431.5 14.8 %collective-permute-start = (bf16[32,8192]{1,0:T(8,128)(2,1)}, bf16[32,8192]{1,0:T(8,128)(2,1)S(1)}, u32[]{:S(2)}, u32[]{:S(2)}) collective-permute-start(bf16[32,8192]{1,0:T(8,128)(2,1)} %copy-done), channel_id=1, source_target_pairs={{0,8},{8,16},{16,24},{1,9},{9,17},{17,25},{2,10},{10,18},{18,26},{... | collective-permute-start | bytes 1572872 | tf_op jit(solution)/shard_map/while/body/eval_jaxpr/ppermute | solution.py:23
  469.7 0.8 copy-start
  470.5 13.9 %collective-permute-start = (bf16[32,8192]{1,0:T(8,128)(2,1)}, bf16[32,8192]{1,0:T(8,128)(2,1)S(1)}, u32[]{:S(2)}, u32[]{:S(2)}) collective-permute-start(bf16[32,8192]{1,0:T(8,128)(2,1)} %copy-done), channel_id=1, source_target_pairs={{0,8},{8,16},{16,24},{1,9},{9,17},{17,25},{2,10},{10,18},{18,26},{... | collective-permute-start | bytes 1572872 | tf_op jit(solution)/shard_map/while/body/eval_jaxpr/ppermute | solution.py:23
  489.6 0.8 copy-start
  490.4 31.8 %collective-permute-start = (bf16[32,8192]{1,0:T(8,128)(2,1)}, bf16[32,8192]{1,0:T(8,128)(2,1)S(1)}, u32[]{:S(2)}, u32[]{:S(2)}) collective-permute-start(bf16[32,8192]{1,0:T(8,128)(2,1)} %copy-done), channel_id=1, source_target_pairs={{0,8},{8,16},{16,24},{1,9},{9,17},{17,25},{2,10},{10,18},{18,26},{... | collective-permute-start | bytes 1572872 | tf_op jit(solution)/shard_map/while/body/eval_jaxpr/ppermute | solution.py:23
  527.5 0.8 copy-start
  528.2 13.2 %collective-permute-start = (bf16[32,8192]{1,0:T(8,128)(2,1)}, bf16[32,8192]{1,0:T(8,128)(2,1)S(1)}, u32[]{:S(2)}, u32[]{:S(2)}) collective-permute-start(bf16[32,8192]{1,0:T(8,128)(2,1)} %copy-done), channel_id=1, source_target_pairs={{0,8},{8,16},{16,24},{1,9},{9,17},{17,25},{2,10},{10,18},{18,26},{... | collective-permute-start | bytes 1572872 | tf_op jit(solution)/shard_map/while/body/eval_jaxpr/ppermute | solution.py:23
  546.7 0.8 copy-start
  547.5 30.5 %collective-permute-start = (bf16[32,8192]{1,0:T(8,128)(2,1)}, bf16[32,8192]{1,0:T(8,128)(2,1)S(1)}, u32[]{:S(2)}, u32[]{:S(2)}) collective-permute-start(bf16[32,8192]{1,0:T(8,128)(2,1)} %copy-done), channel_id=1, source_target_pairs={{0,8},{8,16},{16,24},{1,9},{9,17},{17,25},{2,10},{10,18},{18,26},{... | collective-permute-start | bytes 1572872 | tf_op jit(solution)/shard_map/while/body/eval_jaxpr/ppermute | solution.py:23
  581.8 12.5 %collective-permute-start.1 = (bf16[32,8192]{1,0:T(8,128)(2,1)}, bf16[32,8192]{1,0:T(8,128)(2,1)S(1)}, u32[]{:S(2)}, u32[]{:S(2)}) collective-permute-start(bf16[32,8192]{1,0:T(8,128)(2,1)} %get-tuple-element.1013), channel_id=1, source_target_pairs={{8,0},{16,8},{24,16},{9,1},{17,9},{25,17},{10,2},{18,10},{26,18},{... | collective-permute-start | bytes 1572872 | tf_op jit(solution)/shard_map/while/body/eval_jaxpr/ppermute | solution.py:23
  597.4 27.1 %collective-permute-start.1 = (bf16[32,8192]{1,0:T(8,128)(2,1)}, bf16[32,8192]{1,0:T(8,128)(2,1)S(1)}, u32[]{:S(2)}, u32[]{:S(2)}) collective-permute-start(bf16[32,8192]{1,0:T(8,128)(2,1)} %get-tuple-element.1013), channel_id=1, source_target_pairs={{8,0},{16,8},{24,16},{9,1},{17,9},{25,17},{10,2},{18,10},{26,18},{... | collective-permute-start | bytes 1572872 | tf_op jit(solution)/shard_map/while/body/eval_jaxpr/ppermute | solution.py:23
  627.6 100.3 %collective-permute-start.1 = (bf16[32,8192]{1,0:T(8,128)(2,1)}, bf16[32,8192]{1,0:T(8,128)(2,1)S(1)}, u32[]{:S(2)}, u32[]{:S(2)}) collective-permute-start(bf16[32,8192]{1,0:T(8,128)(2,1)} %get-tuple-element.1013), channel_id=1, source_target_pairs={{8,0},{16,8},{24,16},{9,1},{17,9},{25,17},{10,2},{18,10},{26,18},{... | collective-permute-start | bytes 1572872 | tf_op jit(solution)/shard_map/while/body/eval_jaxpr/ppermute | solution.py:23
  729.7 9.0 copy-start.2
  738.7 10.9 %copy-start.3 = (f32[1,8192]{1,0:T(1,128)S(1)}, f32[1,8192]{1,0:T(1,128)}, u32[]{:S(2)}) copy-start(f32[1,8192]{1,0:T(1,128)} %get-tuple-element.515) | copy-start | bytes 98308 | tf_op jit(solution)/shard_map/while/body/eval_jaxpr/cond
  760.6 12.2 %collective-permute-start.1 = (bf16[32,8192]{1,0:T(8,128)(2,1)}, bf16[32,8192]{1,0:T(8,128)(2,1)S(1)}, u32[]{:S(2)}, u32[]{:S(2)}) collective-permute-start(bf16[32,8192]{1,0:T(8,128)(2,1)} %get-tuple-element.1013), channel_id=1, source_target_pairs={{8,0},{16,8},{24,16},{9,1},{17,9},{25,17},{10,2},{18,10},{26,18},{... | collective-permute-start | bytes 1572872 | tf_op jit(solution)/shard_map/while/body/eval_jaxpr/ppermute | solution.py:23
  774.7 9.0 copy-start.2
  783.7 10.9 %copy-start.3 = (f32[1,8192]{1,0:T(1,128)S(1)}, f32[1,8192]{1,0:T(1,128)}, u32[]{:S(2)}) copy-start(f32[1,8192]{1,0:T(1,128)} %get-tuple-element.515) | copy-start | bytes 98308 | tf_op jit(solution)/shard_map/while/body/eval_jaxpr/cond
  805.6 12.2 %collective-permute-start.1 = (bf16[32,8192]{1,0:T(8,128)(2,1)}, bf16[32,8192]{1,0:T(8,128)(2,1)S(1)}, u32[]{:S(2)}, u32[]{:S(2)}) collective-permute-start(bf16[32,8192]{1,0:T(8,128)(2,1)} %get-tuple-element.1013), channel_id=1, source_target_pairs={{8,0},{16,8},{24,16},{9,1},{17,9},{25,17},{10,2},{18,10},{26,18},{... | collective-permute-start | bytes 1572872 | tf_op jit(solution)/shard_map/while/body/eval_jaxpr/ppermute | solution.py:23
  819.7 9.0 copy-start.2
  828.7 10.9 %copy-start.3 = (f32[1,8192]{1,0:T(1,128)S(1)}, f32[1,8192]{1,0:T(1,128)}, u32[]{:S(2)}) copy-start(f32[1,8192]{1,0:T(1,128)} %get-tuple-element.515) | copy-start | bytes 98308 | tf_op jit(solution)/shard_map/while/body/eval_jaxpr/cond
  850.6 12.2 %collective-permute-start.1 = (bf16[32,8192]{1,0:T(8,128)(2,1)}, bf16[32,8192]{1,0:T(8,128)(2,1)S(1)}, u32[]{:S(2)}, u32[]{:S(2)}) collective-permute-start(bf16[32,8192]{1,0:T(8,128)(2,1)} %get-tuple-element.1013), channel_id=1, source_target_pairs={{8,0},{16,8},{24,16},{9,1},{17,9},{25,17},{10,2},{18,10},{26,18},{... | collective-permute-start | bytes 1572872 | tf_op jit(solution)/shard_map/while/body/eval_jaxpr/ppermute | solution.py:23
  864.7 9.0 copy-start.2
  873.6 10.9 %copy-start.3 = (f32[1,8192]{1,0:T(1,128)S(1)}, f32[1,8192]{1,0:T(1,128)}, u32[]{:S(2)}) copy-start(f32[1,8192]{1,0:T(1,128)} %get-tuple-element.515) | copy-start | bytes 98308 | tf_op jit(solution)/shard_map/while/body/eval_jaxpr/cond
  895.5 11.3 %collective-permute-start.1 = (bf16[32,8192]{1,0:T(8,128)(2,1)}, bf16[32,8192]{1,0:T(8,128)(2,1)S(1)}, u32[]{:S(2)}, u32[]{:S(2)}) collective-permute-start(bf16[32,8192]{1,0:T(8,128)(2,1)} %get-tuple-element.1013), channel_id=1, source_target_pairs={{8,0},{16,8},{24,16},{9,1},{17,9},{25,17},{10,2},{18,10},{26,18},{... | collective-permute-start | bytes 1572872 | tf_op jit(solution)/shard_map/while/body/eval_jaxpr/ppermute | solution.py:23
  906.8 32.1 %copy-start.8 = (s32[64]{0:T(128)S(1)}, s32[64]{0:T(128)}, u32[]{:S(2)}) copy-start(s32[64]{0:T(128)} %copy-done.7) | copy-start | bytes 772
  906.8 32.1 %copy-start.11 = (s32[8]{0:T(128)S(1)}, s32[8]{0:T(128)}, u32[]{:S(2)}) copy-start(s32[8]{0:T(128)} %param.27) | copy-start | bytes 100
  906.8 32.1 %copy-start.13 = (pred[64]{0:T(512)(128)(4,1)S(1)}, pred[64]{0:T(512)(128)(4,1)}, u32[]{:S(2)}) copy-start(pred[64]{0:T(512)(128)(4,1)} %copy-done.12) | copy-start | bytes 196
  906.8 32.1 %copy-start.14 = (pred[64]{0:T(512)(128)(4,1)S(1)}, pred[64]{0:T(512)(128)(4,1)}, u32[]{:S(2)}) copy-start(pred[64]{0:T(512)(128)(4,1)} %get-tuple-element.797) | copy-start | bytes 196
  918.1 20.2 %all-to-all-start.1 = ((bf16[8,2,18432]{2,1,0:T(2,128)(2,1)}), bf16[8,2,18432]{2,1,0:T(2,128)(2,1)S(1)}, u32[]{:S(2)}, u32[]{:S(2)}) async-start(bf16[8,2,18432]{2,1,0:T(2,128)(2,1)} %reshape.278), calls=%async_computation.1 | async-start | bytes 1179648 | tf_op jit(solution)/shard_map/all_to_all | solution.py:291
  955.1 2.2 copy-start.1
  960.3 21.4 %all-to-all-start.2 = ((bf16[8,2,18432]{2,1,0:T(2,128)(2,1)}), bf16[8,2,18432]{2,1,0:T(2,128)(2,1)S(1)}, u32[]{:S(2)}, u32[]{:S(2)}) async-start(bf16[8,2,18432]{2,1,0:T(2,128)(2,1)} %reshape.280), calls=%async_computation.2 | async-start | bytes 1179648 | tf_op jit(solution)/shard_map/all_to_all | solution.py:311
  964.1 18.8 %copy-start.5 = (s32[4]{0:T(128)S(1)}, s32[4]{0:T(128)}, u32[]{:S(2)}) copy-start(s32[4]{0:T(128)} %copy-done.4) | copy-start | bytes 52
Sparse Core Ops, SparseCore 0:
  9.6 166.3 all-gather.2
  177.6 149.2 all-gather.4
where the time goes:
time: 997 us; the launch traced here: 993 us
  waiting for transfers between devices  489 us (49%)
  matrix products  188 us (19%)
  other arithmetic  118 us (12%)
  starting transfers between devices  88.5 us (9%)
  local copies, waits for them, and re-layouts  84.7 us (8%)
  between operations  14.3 us (1%)
  loops' own time  10.6 us (1%)
    ppermute x14, waiting for transfers between devices, from_behind(): return lax.ppermute(shard, axis, pairs)  179 us
    all_gather x1, waiting for transfers between devices, on_device(): lax.all_gather(output_projection_weight, 'dp', axis=1, tiled=True)  151 us
    all_gather x1, waiting for transfers between devices, on_device(): lax.all_gather(value_projection_weight, 'dp', axis=1, tiled=True)  111 us
    dot_general x16, matrix products, contract_trailing(): lax.dot_general(left, right, (((1,), (1,)), ((), ())), preferred_element_...  105 us
    ppermute x14, starting transfers between devices, from_behind(): return lax.ppermute(shard, axis, pairs)  74.7 us
    dot_general x4, matrix products, layer_reverse_pass(): jnp.dot(output_gradient, output_complete, preferred_element_type=jnp.floa...  35.7 us
    all_to_all x1, waiting for transfers between devices, on_device(): lax.all_to_all(hand_out(slot_adapter_params[0]), 'dp', split_axis=0, conc...  31.7 us
    scatter-add x7, other arithmetic, backward_step(): block_grads.at[block_slot_index].add(jnp.where(is_valid, grad_term, 0.0))  31 us
  transfers between devices with their start and end apart: 19, of which 18 were waited for; matrix products, arithmetic and copies ran while one was open for 11% of the time, Pallas kernels for 0%

commit v1 on v0

v1 whole, which is shorter than its diff:
```python
import functools

import jax
import jax.numpy as jnp
from jax import lax
from jax.experimental import pallas as pl
from jax.experimental.pallas import tpu as pltpu
from jax.sharding import PartitionSpec as P

ADAPTER_RANK = 16
MROWS = 16
LANES = 128


ADAPTER_SCALE = 2.0
LEARN_RATE = 0.001
BETA_FIRST = 0.9
BETA_SECOND = 0.999
ADAM_EPS = 1e-08
FIRST_FIX = 1.0 - 0.9**50 * 0.9**50
SECOND_FIX = 1.0 - 0.999**50 * 0.999**50
NORM_EPS = 1e-05
MESH = pl.DeviceIdType.MESH
BF = jnp.bfloat16
F32 = jnp.float32


def dot_nt(left, right):
    return lax.dot_general(left, right, (((1,), (1,)), ((), ())), preferred_element_type=F32)


def dot_tn(left, right):
    return lax.dot_general(left, right, (((0,), (0,)), ((), ())), preferred_element_type=F32)


def dot_nn(left, right):
    return jnp.dot(left, right, preferred_element_type=F32)


def layers_kernel(
    dims,
    tok,
    cot,
    gain,
    vw,
    ow,
    aw,
    bw,
    mask,
    fold,
    h,
    val,
    gv,
    gl,
    dh,
    snd_f,
    pr_f,
    mid_f,
    rs_f,
    snd_b,
    pr_b,
    mid_b,
    rs_b,
    h_out,
    dh_out,
    sem_f,
    sem_b,
    h_sem,
    dh_sem,
    tok_sem,
    cot_sem,
    send_sem,
):
    sections, n, micros, q, features, width = dims
    hz = n // 2
    rows = n * q
    half = rows // 2
    hidden = n * width
    s = lax.axis_index("section")
    j = lax.axis_index("dp")
    z = j // 2
    c = lax.rem(j, 2)
    peer = j + 1 - 2 * c
    last = sections - 1

    barrier = pltpu.get_barrier_semaphore()

    def greet(k, carry):
        pl.semaphore_signal(
            barrier, inc=1, device_id={"dp": lax.rem(j + k, n)}, device_id_type=MESH
        )
        return carry

    lax.fori_loop(1, n, greet, 0)

    @pl.when(s > 0)
    def _():
        pl.semaphore_signal(barrier, inc=1, device_id={"section": s - 1}, device_id_type=MESH)

    @pl.when(s < last)
    def _():
        pl.semaphore_signal(barrier, inc=1, device_id={"section": s + 1}, device_id_type=MESH)

    beside = jnp.where(s > 0, 1, 0) + jnp.where(s < last, 1, 0)
    pl.semaphore_wait(barrier, n - 1 + beside)

    def remote(source, target, send, recv, device):
        return pltpu.make_async_remote_copy(
            src_ref=source,
            dst_ref=target,
            send_sem=send,
            recv_sem=recv,
            device_id=device,
            device_id_type=MESH,
        )

    def wait_bytes(ref, sem):
        pltpu.make_async_copy(ref, ref, sem).wait()

    def spread(source, target, sem, sent, m):
        mine = pl.ds(pl.multiple_of(m * q, q), q)
        place = pl.ds(pl.multiple_of(j * q, q), q)

        def one(k, carry):
            to = lax.rem(j + k, n)
            columns = pl.ds(pl.multiple_of(to * width, width), width)
            remote(
                source.at[mine, columns], target.at[m, place], sent, sem.at[m], {"dp": to}
            ).start()
            return carry

        lax.fori_loop(1, n, one, 0)
        target[m, place, :] = source[mine, pl.ds(pl.multiple_of(j * width, width), width)]

    def spread_wait(target, sem, m):
        wait_bytes(target.at[m, pl.ds(0, (n - 1) * q)], sem.at[m])

    class Reduce:
        def __init__(self, snd, pr, mid, rs, out, sem, middle, finish):
            self.snd, self.pr, self.mid, self.rs = snd, pr, mid, rs
            self.out, self.sem, self.middle, self.finish = out, sem, middle, finish
            self.own = pl.ds(pl.multiple_of(c * half, half), half)
            self.other = pl.ds(pl.multiple_of((1 - c) * half, half), half)
            self.chunk = pl.ds(pl.multiple_of(c * half + z * q, q), q)

        def pair(self):
            return remote(
                self.snd.at[self.other], self.pr, self.sem.at[0], self.sem.at[1], {"dp": peer}
            )

        def scatter(self):
            self.pair().wait_recv()
            total = self.snd[self.own, :].astype(F32) + self.pr[...].astype(F32)
            self.mid[...] = self.middle(total)
            for k in range(1, hz):
                to = lax.rem(z + k, hz)
                remote(
                    self.mid.at[pl.ds(pl.multiple_of(to * q, q), q)],
                    self.rs.at[z],
                    self.sem.at[2],
                    self.sem.at[3],
                    {"dp": 2 * to + c},
                ).start()
            self.rs[z] = self.mid[pl.ds(pl.multiple_of(z * q, q), q), :]

        def gather(self, m):
            if hz > 1:
                wait_bytes(self.rs.at[pl.ds(0, hz - 1)], self.sem.at[3])
            total = self.rs[0].astype(F32)
            for k in range(1, hz):
                total = total + self.rs[k].astype(F32)
            self.out[m, self.chunk, :] = self.finish(total)
            for k in range(1, hz):
                to = lax.rem(z + k, hz)
                remote(
                    self.out.at[m, self.chunk],
                    self.out.at[m, self.chunk],
                    self.sem.at[4],
                    self.sem.at[5],
                    {"dp": 2 * to + c},
                ).start()

        def share(self, m):
            if hz > 1:
                wait_bytes(self.out.at[m, pl.ds(0, (hz - 1) * q)], self.sem.at[5])
            remote(
                self.out.at[m, self.own],
                self.out.at[m, self.own],
                self.sem.at[6],
                self.sem.at[7],
                {"dp": peer},
            ).start()

        def arrive(self, m):
            wait_bytes(self.out.at[m, pl.ds(0, half)], self.sem.at[7])

        def drain(self, m):
            self.pair().wait_send()
            if hz > 1:
                wait_bytes(self.mid.at[pl.ds(0, (hz - 1) * q)], self.sem.at[2])
                wait_bytes(self.out.at[m, pl.ds(0, (hz - 1) * q)], self.sem.at[4])
            wait_bytes(self.out.at[m, pl.ds(0, half)], self.sem.at[6])

    def with_stat(tail, stat):
        spot = lax.broadcasted_iota(jnp.int32, tail.shape, 1)
        high = stat.astype(BF).astype(F32)
        rest = stat - high
        return jnp.where(
            spot < ADAPTER_RANK,
            tail,
            jnp.where(
                spot == ADAPTER_RANK, high, jnp.where(spot == ADAPTER_RANK + 1, rest, 0.0)
            ),
        ).astype(BF)

    def stat_of(tail):
        spot = lax.broadcasted_iota(jnp.int32, tail.shape, 1)
        inside = (spot == ADAPTER_RANK) | (spot == ADAPTER_RANK + 1)
        return jnp.sum(jnp.where(inside, tail, 0.0), axis=1, keepdims=True)

    def middle_f(total):
        tail = total[:, features:]
        return jnp.concatenate(
            [total[:, :features].astype(BF), with_stat(tail, stat_of(tail))], axis=1
        )

    def finish_f(total):
        tail = total[:, features:]
        scale = lax.rsqrt(stat_of(tail) / hidden + NORM_EPS)
        return jnp.concatenate(
            [(total[:, :features] * scale).astype(BF), with_stat(tail * scale, scale)], axis=1
        )

    def plain(total):
        return total.astype(BF)

    ahead = Reduce(snd_f, pr_f, mid_f, rs_f, val, sem_f, middle_f, finish_f)
    back = Reduce(snd_b, pr_b, mid_b, rs_b, gv, sem_b, plain, plain)

    def wide_low(tail):
        spread_low = dot_nt(tail, fold[...])
        return jnp.where(mask[...] > 0, spread_low, 0.0).astype(BF)

    def ahead_start(m):
        @pl.when(s == 0)
        def _():
            spread_wait(h, tok_sem, m)

        @pl.when(s > 0)
        def _():
            wait_bytes(h.at[m], h_sem.at[m])

        wide = h[m].astype(F32)
        scaled = (wide * gain[...]).astype(BF)
        snd_f[:, :features] = dot_nn(scaled, vw[...]).astype(BF)
        low = jnp.where(mask[...] > 0, dot_nn(scaled, aw[...]), 0.0).astype(BF)
        squares = jnp.sum(wide * wide, axis=1, keepdims=True)
        snd_f[:, features:] = with_stat(dot_nn(low, fold[...]), squares)
        ahead.pair().start()

    def ahead_end(m):
        ahead.arrive(m)

        @pl.when(s < last)
        def _():
            low = wide_low(val[m, :, features:])
            value = (
                val[m, :, :features].astype(F32) + ADAPTER_SCALE * dot_nn(low, bw[...])
            ).astype(BF)
            result = (h[m].astype(F32) + dot_nt(value, ow[...])).astype(BF)

            @pl.when(m > 0)
            def _():
                wait_bytes(h_out, send_sem.at[0])

            h_out[...] = result
            remote(
                h_out, h.at[m], send_sem.at[0], h_sem.at[m], {"section": s + 1}
            ).start()

        ahead.drain(m)

    def back_start(m):
        @pl.when(s == last)
        def _():
            spread_wait(dh, cot_sem, m)

        @pl.when(s < last)
        def _():
            wait_bytes(dh.at[m], dh_sem.at[m])

        snd_b[...] = dot_nn(dh[m], ow[...]).astype(BF)
        back.pair().start()

    def back_end(m):
        back.arrive(m)
        grad_value = gv[m]
        grad_low = jnp.where(
            mask[...] > 0, ADAPTER_SCALE * dot_nt(grad_value, bw[...]), 0.0
        ).astype(BF)
        gl[m] = grad_low

        @pl.when(s > 0)
        def _():
            tail = val[m, :, features:]
            scale = stat_of(tail.astype(F32))
            low = wide_low(tail)
            inner = jnp.sum(
                grad_value.astype(F32) * val[m, :, :features].astype(F32), axis=1, keepdims=True
            ) + jnp.sum(grad_low.astype(F32) * low.astype(F32), axis=1, keepdims=True)
            norm_grad = (dot_nt(grad_value, vw[...]) + dot_nt(grad_low, aw[...])) * gain[...]
            result = (
                dh[m].astype(F32)
                + scale * norm_grad
                - h[m].astype(F32) * (scale * scale * inner / hidden)
            ).astype(BF)

            @pl.when(m > 0)
            def _():
                wait_bytes(dh_out, send_sem.at[1])

            dh_out[...] = result
            remote(
                dh_out, dh.at[m], send_sem.at[1], dh_sem.at[m], {"section": s - 1}
            ).start()

        back.drain(m)

    @pl.when(s == 0)
    def _():
        for m in range(min(2, micros)):
            spread(tok, h, tok_sem, send_sem.at[2], m)

    def step(t, carry):
        m_f = t - s
        m_b = t - (2 * sections - 1 - s)
        on_f = (m_f >= 0) & (m_f < micros)
        on_b = (m_b >= 0) & (m_b < micros)

        @pl.when((s == 0) & (t + 2 < micros))
        def _():
            spread(tok, h, tok_sem, send_sem.at[2], t + 2)

        @pl.when((s == last) & (t < micros))
        def _():
            spread(cot, dh, cot_sem, send_sem.at[3], t)

        pl.when(on_b)(lambda: back_start(m_b))
        pl.when(on_f)(lambda: ahead_start(m_f))
        pl.when(on_b)(lambda: back.scatter())
        pl.when(on_f)(lambda: ahead.scatter())
        pl.when(on_b)(lambda: back.gather(m_b))
        pl.when(on_f)(lambda: ahead.gather(m_f))
        pl.when(on_b)(lambda: back.share(m_b))
        pl.when(on_f)(lambda: ahead.share(m_f))
        pl.when(on_b)(lambda: back_end(m_b))
        pl.when(on_f)(lambda: ahead_end(m_f))
        return carry

    lax.fori_loop(0, micros + 2 * sections - 1, step, 0)

    @pl.when(s < last)
    def _():
        wait_bytes(h_out, send_sem.at[0])

    @pl.when(s > 0)
    def _():
        wait_bytes(dh_out, send_sem.at[1])

    @pl.when(s == 0)
    def _():
        wait_bytes(tok.at[:, pl.ds(0, (n - 1) * width)], send_sem.at[2])

    @pl.when(s == last)
    def _():
        wait_bytes(cot.at[:, pl.ds(0, (n - 1) * width)], send_sem.at[3])


def run_layers(tokens, cotangent, gain, vw, ow, aw, bw, mask, fold):
    sections, n = lax.axis_size("section"), lax.axis_size("dp")
    q = MROWS
    width, features = vw.shape
    ranks = aw.shape[1]
    micros = tokens.shape[0] // q
    rows = n * q
    wide = features + LANES
    vmem = pl.BlockSpec(memory_space=pltpu.VMEM)
    dma = pltpu.SemaphoreType.DMA
    dims = (sections, n, micros, q, features, width)
    return pl.pallas_call(
        functools.partial(layers_kernel, dims),
        out_shape=(
            jax.ShapeDtypeStruct((micros, rows, width), BF),
            jax.ShapeDtypeStruct((micros, rows, wide), BF),
            jax.ShapeDtypeStruct((micros, rows, features), BF),
            jax.ShapeDtypeStruct((micros, rows, ranks), BF),
        ),
        in_specs=[vmem] * 9,
        out_specs=(vmem,) * 4,
        scratch_shapes=[
            pltpu.VMEM((micros, rows, width), BF),
            pltpu.VMEM((rows, wide), BF),
            pltpu.VMEM((rows // 2, wide), BF),
            pltpu.VMEM((rows // 2, wide), BF),
            pltpu.VMEM((n // 2, q, wide), BF),
            pltpu.VMEM((rows, features), BF),
            pltpu.VMEM((rows // 2, features), BF),
            pltpu.VMEM((rows // 2, features), BF),
            pltpu.VMEM((n // 2, q, features), BF),
            pltpu.VMEM((rows, width), BF),
            pltpu.VMEM((rows, width), BF),
            dma((8,)),
            dma((8,)),
            dma((micros,)),
            dma((micros,)),
            dma((micros,)),
            dma((micros,)),
            dma((4,)),
        ],
        compiler_params=pltpu.CompilerParams(
            collective_id=0, has_side_effects=True, vmem_limit_bytes=58 * 1024 * 1024
        ),
    )(tokens, cotangent, gain, vw, ow, aw, bw, mask, fold)


def adam_update(params_old, first_old, second_old, slot_grad, live):
    first_step = BETA_FIRST * first_old + (1.0 - BETA_FIRST) * slot_grad
    second_step = BETA_SECOND * second_old + (1.0 - BETA_SECOND) * slot_grad * slot_grad
    step_size = first_step / FIRST_FIX / (jnp.sqrt(second_step / SECOND_FIX) + ADAM_EPS)
    params_step = (params_old.astype(jnp.float32) - LEARN_RATE * step_size).astype(jnp.bfloat16)
    return (
        jnp.where(live, params_step, params_old),
        jnp.where(live, first_step, first_old),
        jnp.where(live, second_step, second_old),
    )


def on_device(
    tokens,
    cotangent,
    gains,
    value_projection_weight,
    output_projection_weight,
    block_adapter_ids,
    job_adapter,
    job_slab,
    token_counts,
    slot_adapter_params,
    first_moment,
    second_moment,
):
    section_index = lax.axis_index("section")
    owner_index = lax.axis_index("dp")
    section_total = lax.axis_size("section")
    owner_total = lax.axis_size("dp")
    tok_dev, hidden_width = tokens.shape
    value_feature_width = value_projection_weight.shape[2]
    panel_width = slot_adapter_params.shape[2]
    slab_count = owner_total // 2
    block_total = block_adapter_ids.shape[0]
    local_blocks = block_total // owner_total
    block_rows = tok_dev // local_blocks
    adapter_total = token_counts.shape[0]
    divide_position = hidden_width * ADAPTER_RANK
    width = hidden_width // owner_total
    gain = lax.dynamic_slice_in_dim(gains, owner_index * width, width, axis=1)
    my_jobs = lax.dynamic_index_in_dim(job_adapter, owner_index, 0, keepdims=False)
    my_blocks = lax.dynamic_slice_in_dim(
        block_adapter_ids, owner_index * local_blocks, local_blocks
    )
    slab_ids = jnp.arange(slab_count, dtype=jnp.int32)
    matching = (job_adapter[None, None] == my_blocks[:, None, None, None]) & (
        job_slab[None, None] == slab_ids[None, :, None, None]
    )
    owner_ids = jnp.arange(owner_total, dtype=jnp.int32)
    source_owner = jnp.sum(jnp.where(matching, owner_ids[None, None, :, None], 0), axis=(2, 3))
    own_select = (block_adapter_ids[:, None] == my_jobs[None, :]) & (my_jobs[None, :] >= 0)
    slot_rows = jnp.arange(local_blocks, dtype=jnp.int32)[:, None]

    def hand_out(owned):
        picked = jnp.dot(own_select.astype(jnp.bfloat16), owned, preferred_element_type=jnp.float32)
        return picked.astype(jnp.bfloat16).reshape(owner_total, local_blocks, panel_width)

    def assemble(arrived):
        gathered_slabs = arrived[source_owner, slot_rows]
        return gathered_slabs.reshape(local_blocks, slab_count * panel_width)

    ranks = block_total * ADAPTER_RANK
    my_slabs = lax.dynamic_index_in_dim(job_slab, owner_index, 0, keepdims=False)
    held_slab = jnp.max(jnp.where(own_select, my_slabs[None, :], -1), axis=1)
    held = held_slab[:, None] == slab_ids[None, :]
    picked = hand_out(slot_adapter_params[0]).reshape(block_total, 1, panel_width)
    padded = jnp.where(held[:, :, None], picked, jnp.zeros((), BF)).reshape(
        block_total, slab_count * panel_width
    )
    down_part = jnp.transpose(
        padded[:, :divide_position].reshape(block_total, owner_total, width * ADAPTER_RANK),
        (1, 0, 2),
    )
    adapter_down = lax.psum_scatter(down_part, "dp", scatter_dimension=0, tiled=False)
    adapter_up = lax.psum(padded[:, divide_position:], "dp").reshape(ranks, value_feature_width)
    adapter_down = jnp.transpose(
        adapter_down.reshape(block_total, width, ADAPTER_RANK), (1, 0, 2)
    ).reshape(width, ranks)
    rows = owner_total * MROWS
    mask = (
        jnp.arange(rows, dtype=jnp.int32)[:, None] // MROWS
        == jnp.arange(ranks, dtype=jnp.int32)[None, :] // ADAPTER_RANK
    )
    fold = (
        jnp.arange(ranks, dtype=jnp.int32)[:, None] % ADAPTER_RANK
        == jnp.arange(LANES, dtype=jnp.int32)[None, :]
    ).astype(BF)
    hidden, val, grad_value, grad_low = run_layers(
        tokens,
        cotangent,
        gain,
        value_projection_weight[0],
        output_projection_weight[0],
        adapter_down,
        adapter_up,
        mask.astype(F32),
        fold,
    )
    total_rows = hidden.shape[0] * rows
    tail = val[:, :, value_feature_width:]
    scale = tail[:, :, ADAPTER_RANK].astype(F32) + tail[:, :, ADAPTER_RANK + 1].astype(F32)
    normed = (hidden.astype(F32) * scale[:, :, None] * gain[0]).astype(BF)
    low = jnp.where(
        mask, jnp.tile(tail[:, :, :ADAPTER_RANK], (1, 1, block_total)), jnp.zeros((), BF)
    )
    down_grads = dot_tn(
        normed.reshape(total_rows, width), grad_low.reshape(total_rows, ranks)
    ).astype(BF)
    up_grads = (
        ADAPTER_SCALE
        * dot_tn(
            low.reshape(total_rows, ranks), grad_value.reshape(total_rows, value_feature_width)
        )
    ).astype(BF)
    down_grads = jnp.transpose(
        down_grads.reshape(width, block_total, ADAPTER_RANK), (1, 0, 2)
    ).reshape(block_total, width * ADAPTER_RANK)
    down_grads = lax.all_gather(down_grads, "dp", axis=1, tiled=True)
    block_grads = jnp.concatenate(
        [down_grads, up_grads.reshape(block_total, ADAPTER_RANK * value_feature_width)], axis=1
    ).reshape(block_total, slab_count, panel_width)
    arrived = jnp.sum(
        jnp.where(held[:, :, None], block_grads.astype(F32), 0.0), axis=1
    ).astype(BF)
    summed = dot_tn(own_select.astype(BF), arrived)
    live = my_jobs >= 0
    adapter_ids = jnp.arange(adapter_total, dtype=jnp.int32)
    slot_counts = jnp.sum(
        jnp.where(adapter_ids[None, :] == my_jobs[:, None], token_counts[None, :], 0), axis=1
    )
    slot_counts = jnp.where(live, slot_counts, 1)
    slot_grad = summed / slot_counts.astype(jnp.float32)[:, None]
    params_new, first_new, second_new = adam_update(
        slot_adapter_params[0], first_moment[0], second_moment[0], slot_grad, live[:, None]
    )
    returned = assemble(
        lax.all_to_all(hand_out(params_new), "dp", split_axis=0, concat_axis=0, tiled=True)
    )
    return (params_new[None], first_new[None], second_new[None], returned[None])


def solution(mesh):
    return jax.shard_map(
        on_device,
        mesh=mesh,
        in_specs=(
            P("dp", None),
            P("dp", None),
            P("section", None),
            P("section", "dp", None),
            P("section", "dp", None),
            P(),
            P(),
            P(),
            P(),
            P("section", "dp", None),
            P("section", "dp", None),
            P("section", "dp", None),
        ),
        out_specs=(
            P("section", "dp", None),
            P("section", "dp", None),
            P("section", "dp", None),
            P("section", "dp", None),
        ),
        check_vma=False,
    )
```

time: 997 us -> 561 us (0.56)
  waiting for transfers between devices: 489 us -> 111 us
  Pallas kernels: 0 us -> 353 us
  matrix products: 188 us -> 24.8 us
  other arithmetic: 118 us -> 30.5 us
  starting transfers between devices: 88.5 us -> 3.66 us
  local copies, waits for them, and re-layouts: 84.7 us -> 23.5 us
  loops' own time: 10.6 us -> 0 us
    pallas_call x0 -> x1, Pallas kernels: none -> 353 us  [run_layers(): pl.pallas_call(functools.partial(layers_kernel, dims), out_shape=(jax.Sha...]
    all_gather x2 -> x1, waiting for transfers between devices: 262 us -> 22.2 us  [on_device(): down_grads = lax.all_gather(down_grads, 'dp', axis=1, tiled=True)]
    ppermute x14 -> x0, waiting for transfers between devices: 179 us -> none  [from_behind(): return lax.ppermute(shard, axis, pairs)]
    dot_general x37 -> x3, matrix products: 184 us -> 20.9 us  [dot_tn(): lax.dot_general(left, right, (((0,), (0,)), ((), ())), preferred_element_...]
    ppermute x14 -> x0, starting transfers between devices: 74.7 us -> none  [from_behind(): return lax.ppermute(shard, axis, pairs)]
    psum x0 -> x1, waiting for transfers between devices: none -> 52.4 us  [on_device(): lax.psum(padded[:, divide_position:], 'dp')]
    all_to_all x2 -> x0, waiting for transfers between devices: 46.8 us -> none  [the longest x1 31.7 us: on_device(): lax.all_to_all(hand_out(slot_adapter_params[0]), 'dp', split_axis=0, conc...]
    reduce_scatter x0 -> x1, waiting for transfers between devices: none -> 36.3 us  [on_device(): lax.psum_scatter(down_part, 'dp', scatter_dimension=0, tiled=False)]
  transfers between devices with their start and end apart: 19 -> 4, of which waited for: 18 -> 3; matrix products, arithmetic and copies ran while one was open for 11% -> 5% of each run, Pallas kernels for 0% -> 0%
where the time goes in v1:
time: 561 us
  Pallas kernels  353 us (63%)
  waiting for transfers between devices  111 us (20%)
  other arithmetic  30.5 us (5%)
  matrix products  24.8 us (4%)
  local copies, waits for them, and re-layouts  23.5 us (4%)
  between operations  14 us (2%)
    pallas_call x1, Pallas kernels, run_layers(): pl.pallas_call(functools.partial(layers_kernel, dims), out_shape=(jax.Sha...  353 us
    psum x1, waiting for transfers between devices, on_device(): lax.psum(padded[:, divide_position:], 'dp')  52.4 us
    reduce_scatter x1, waiting for transfers between devices, on_device(): lax.psum_scatter(down_part, 'dp', scatter_dimension=0, tiled=False)  36.3 us
    all_gather x1, waiting for transfers between devices, on_device(): down_grads = lax.all_gather(down_grads, 'dp', axis=1, tiled=True)  22.2 us
    dot_general x3, matrix products, dot_tn(): lax.dot_general(left, right, (((0,), (0,)), ((), ())), preferred_element_...  20.9 us
    broadcast_in_dim x1, other arithmetic, on_device(): return (params_new[None], first_new[None], second_new[None], returned[None])  17.6 us
  transfers between devices with their start and end apart: 4, of which 3 were waited for; matrix products, arithmetic and copies ran while one was open for 5% of the time, Pallas kernels for 0%

profile of v1, /device:TPU:0, one launch (start us, length us, event | category | flops | bytes accessed | tf_op | source)
XLA Modules:
  0.0 560.8 jit_solution(943795892376175669)
XLA Ops:
  7.2 0.0 reduce-scatter.2.cloned.1.call-start
  7.2 0.7 broadcast_compare_fusion.2
  7.9 0.7 compare_bitcast_fusion
  8.6 0.7 fusion.28
  9.3 0.8 select_reduce_fusion.2
  10.2 3.1 convolution_convert_fusion.1
  13.3 0.3 broadcast_select_fusion
  13.6 1.5 slice.26
  15.1 0.0 all-reduce.3.cloned.1.call-start
  15.1 0.8 reshape.227
  16.0 0.0 all-reduce.3.cloned.1.call-update
  16.0 0.0 all-gather.2.cloned.1.call-start
  16.1 0.7 fusion.27
  16.8 0.6 constant_dynamic-slice_fusion.gain
  17.4 36.3 %reduce-scatter.2.cloned.1.call-done = bf16[1,8,16384]{2,1,0:T(8,128)(2,1)} async-done(((bf16[8,8,16384]{2,1,0:T(8,128)(2,1)}), bf16[1,8,16384]{2,1,0:T(8,128)(2,1)}) %reduce-scatter.2.cloned.1.call-update) | async-done | bytes 262160 | tf_op jit(solution)/shard_map/reduce_scatter | solution.py:500
  53.7 2.5 reshape_reduce_scatter.3
  56.2 0.8 copy.33
  57.0 0.8 copy.34.aw
  57.8 52.4 %all-reduce.3.cloned.1.call-done.bw = bf16[128,1024]{1,0:T(8,128)(2,1)} async-done(((bf16[128,1024]{1,0:T(8,128)(2,1)}), bf16[128,1024]{1,0:T(8,128)(2,1)}) %all-reduce.3.cloned.1.call-update) | async-done | bytes 262160 | tf_op jit(solution)/shard_map/psum | solution.py:501
  110.2 353.3 %shard_map.147 = (bf16[8,128,1024]{2,1,0:T(8,128)(2,1)}, bf16[8,128,1152]{2,1,0:T(8,128)(2,1)}, bf16[8,128,1024]{2,1,0:T(8,128)(2,1)}, bf16[8,128,128]{2,1,0:T(8,128)(2,1)}) custom-call(bf16[128,8192]{1,0:T(8,128)(2,1)} %tok.1, bf16[128,8192]{1,0:T(8,128)(2,1)} %cot.1, f32[1,1024]{1,0:T(1,128)} %constant_dynamic-slice_fusion.gain, ...), custom_call_target="tpu_custom_call" | custom-call | tf_op jit(solution)/shard_map/pallas_call | solution.py:390
  463.5 1.4 add_reduce_fusion
  465.0 2.4 fusion.13
  467.4 1.0 copy.36
  468.4 4.5 reshape.229
  473.0 0.6 dynamic_slice.16
  473.6 0.1 copy.37
  473.7 0.7 broadcast_compare_fusion.1
  474.4 0.2 select_reduce_fusion.1
  474.6 0.2 select_reduce_fusion
  474.8 1.0 slice.23
  475.8 0.1 copy.38
  475.9 2.0 fusion.14
  478.0 0.1 reshape.230
  478.1 22.2 %all-gather.2.cloned.1.call-done = bf16[8,131072]{1,0:T(8,128)(2,1)} async-done(((bf16[8,16384]{1,0:T(8,128)(2,1)}), bf16[8,131072]{1,0:T(8,128)(2,1)}) %all-gather.2.cloned.1.call-update) | async-done | bytes 2097168 | tf_op jit(solution)/shard_map/all_gather | solution.py:544
  500.3 5.6 %pad_maximum_fusion = bf16[8,147456]{1,0:T(8,128)(2,1)S(1)} fusion(bf16[8,16384]{1,0:T(8,128)(2,1)S(1)} %reshape.230, bf16[8,131072]{1,0:T(8,128)(2,1)} %all-gather.2.cloned.1.call-done), kind=kLoop, calls=%fused_computation.20 | loop fusion | flops 4718592 | bytes 4718592 | tf_op jit(solution)/shard_map/concatenate | solution.py:545
  505.9 0.6 fusion.6
  506.5 16.4 %fusion.5 = (bf16[64,36864]{1,0:T(8,128)(2,1)S(1)}, f32[64,36864]{1,0:T(8,128)}) fusion(f32[1,64,36864]{2,1,0:T(8,128)} %param.23, f32[1,64,36864]{2,1,0:T(8,128)} %param.22, bf16[1,64,36864]{2,1,0:T(8,128)(2,1)} %param.21, pred[64]{0:T(512)(128)(4,1)S(1)} %get-tuple-element.12, f32[64]{0:T(128)S(1)} %select_convert_fusion, ...), kind=kOutput, calls=%fused_computation.15 | convolution fusion | flops 77857792 | bytes 38339232 | tf_op jit(solution)/shard_map/dot_general | solution.py:33
  523.0 2.2 copy-done.2
  525.1 0.8 fusion
  525.9 0.5 broadcast.229
  526.4 1.1 reduce.3
  527.5 1.3 reshape.245
  528.8 3.5 all-to-all-start
  532.3 17.6 %fusion.2 = (f32[1,64,36864]{2,1,0:T(8,128)}, f32[1,64,36864]{2,1,0:T(8,128)}) fusion(f32[1,64,36864]{2,1,0:T(8,128)} %param.23, f32[64,36864]{1,0:T(8,128)} %get-tuple-element.19, pred[64]{0:T(512)(128)(4,1)S(1)} %get-tuple-element.12, f32[1,64,36864]{2,1,0:T(8,128)} %param.22), kind=kLoop, calls=%fused_computation.9 | loop fusion | flops 21233664 | bytes 47185984 | tf_op jit(solution)/shard_map/broadcast_in_dim | solution.py:565
  549.9 0.6 reshape.246
  550.5 0.7 copy.40
  551.2 1.9 gather_fusion
  553.1 1.2 broadcast_in_dim_reshape.3
  (27 shorter events, 0.2 us)
Async XLA Ops:
  7.2 9.6 %copy-start = (f32[1,8192]{1,0:T(1,128)S(1)}, f32[1,8192]{1,0:T(1,128)}, u32[]{:S(2)}) copy-start(f32[1,8192]{1,0:T(1,128)} %param.14) | copy-start | bytes 98308
  7.2 46.5 %reduce-scatter.2.cloned.1.call-start = ((), (), s32[]{:S(2)}) async-start(), calls=%async_computation.2 | async-start | bytes 2359296 | tf_op jit(solution)/shard_map/reduce_scatter | solution.py:500
  15.1 95.1 %all-reduce.3.cloned.1.call-start = ((), (), s32[]{:S(2)}) async-start(), calls=%async_computation.3 | async-start | bytes 524288 | tf_op jit(solution)/shard_map/psum | solution.py:501
  16.0 484.3 %all-gather.2.cloned.1.call-start = ((), (), s32[]{:S(2)}) async-start(), calls=%async_computation.4 | async-start | bytes 2359296 | tf_op jit(solution)/shard_map/all_gather | solution.py:544
  110.2 354.7 %copy-start.3 = (f32[1,1024]{1,0:T(1,128)S(1)}, f32[1,1024]{1,0:T(1,128)}, u32[]{:S(2)}) copy-start(f32[1,1024]{1,0:T(1,128)} %constant_dynamic-slice_fusion.gain) | copy-start | bytes 12292
  465.0 8.0 %copy-start.5 = (s32[8]{0:T(128)S(1)}, s32[8]{0:T(128)}, u32[]{:S(2)}) copy-start(s32[8]{0:T(128)} %param.17) | copy-start | bytes 100
  465.0 8.7 %copy-start.4 = (s32[8,64]{1,0:T(8,128)S(1)}, s32[8,64]{1,0:T(8,128)}, u32[]{:S(2)}) copy-start(s32[8,64]{1,0:T(8,128)} %param.18) | copy-start | bytes 6148
  465.0 9.4 %copy-start.6 = (s32[8,64]{1,0:T(8,128)S(1)}, s32[8,64]{1,0:T(8,128)}, u32[]{:S(2)}) copy-start(s32[8,64]{1,0:T(8,128)} %param.19) | copy-start | bytes 6148
  465.0 9.6 %copy-start.7 = (s32[64]{0:T(128)S(1)}, s32[64]{0:T(128)}, u32[]{:S(2)}) copy-start(s32[64]{0:T(128)} %param.20) | copy-start | bytes 772
  523.0 2.2 copy-start.2
  528.8 21.1 %all-to-all-start = ((bf16[8,2,18432]{2,1,0:T(2,128)(2,1)}), bf16[8,2,18432]{2,1,0:T(2,128)(2,1)S(1)}, u32[]{:S(2)}, u32[]{:S(2)}) async-start(bf16[8,2,18432]{2,1,0:T(2,128)(2,1)} %reshape.245), calls=%async_computation.1 | async-start | bytes 1179648 | tf_op jit(solution)/shard_map/all_to_all | solution.py:563
  532.3 21.9 %copy-start.1 = (f32[1,8192]{1,0:T(1,128)S(1)}, f32[1,8192]{1,0:T(1,128)}, u32[]{:S(2)}) copy-start(f32[1,8192]{1,0:T(1,128)} %param.14) | copy-start | bytes 98308
Sparse Core Ops, SparseCore 0:
  15.2 38.4 reduce-scatter.1
  56.6 53.5 all-reduce.2
  473.1 27.1 all-gather.1

commit v2 on v1

--- a/solution.py
+++ b/solution.py
@@ -45,7 +45,7 @@
     vw,
     ow,
     aw,
-    bw,
+    bpart,
     mask,
     fold,
     h,
@@ -53,6 +53,7 @@
     gv,
     gl,
     dh,
+    bw,
     snd_f,
     pr_f,
     mid_f,
@@ -69,6 +70,7 @@
     dh_sem,
     tok_sem,
     cot_sem,
+    up_sem,
     send_sem,
 ):
     sections, n, micros, q, features, width = dims
@@ -331,6 +333,20 @@
         for m in range(min(2, micros)):
             spread(tok, h, tok_sem, send_sem.at[2], m)
 
+    part_rows = bpart.shape[0]
+    up_place = pl.ds(pl.multiple_of(j * part_rows, part_rows), part_rows)
+
+    def send_up(k, carry):
+        remote(
+            bpart, bw.at[up_place], send_sem.at[4], up_sem.at[0], {"dp": lax.rem(j + k, n)}
+        ).start()
+        return carry
+
+    lax.fori_loop(1, n, send_up, 0)
+    bw[up_place, :] = bpart[...]
+    others = bw.at[pl.ds(0, (n - 1) * part_rows)]
+    wait_bytes(others, up_sem.at[0])
+
     def step(t, carry):
         m_f = t - s
         m_b = t - (2 * sections - 1 - s)
@@ -345,19 +361,21 @@
         def _():
             spread(cot, dh, cot_sem, send_sem.at[3], t)
 
+        pl.when(on_f)(lambda: ahead_start(m_f))
+        pl.when(on_f)(lambda: ahead.scatter())
         pl.when(on_b)(lambda: back_start(m_b))
-        pl.when(on_f)(lambda: ahead_start(m_f))
+        pl.when(on_f)(lambda: ahead.gather(m_f))
         pl.when(on_b)(lambda: back.scatter())
-        pl.when(on_f)(lambda: ahead.scatter())
+        pl.when(on_f)(lambda: ahead.share(m_f))
         pl.when(on_b)(lambda: back.gather(m_b))
-        pl.when(on_f)(lambda: ahead.gather(m_f))
+        pl.when(on_f)(lambda: ahead_end(m_f))
         pl.when(on_b)(lambda: back.share(m_b))
-        pl.when(on_f)(lambda: ahead.share(m_f))
         pl.when(on_b)(lambda: back_end(m_b))
-        pl.when(on_f)(lambda: ahead_end(m_f))
         return carry
 
     lax.fori_loop(0, micros + 2 * sections - 1, step, 0)
+
+    wait_bytes(others, send_sem.at[4])
 
     @pl.when(s < last)
     def _():
@@ -399,6 +417,7 @@
         out_specs=(vmem,) * 4,
         scratch_shapes=[
             pltpu.VMEM((micros, rows, width), BF),
+            pltpu.VMEM((ranks, features), BF),
             pltpu.VMEM((rows, wide), BF),
             pltpu.VMEM((rows // 2, wide), BF),
             pltpu.VMEM((rows // 2, wide), BF),
@@ -415,7 +434,8 @@
             dma((micros,)),
             dma((micros,)),
             dma((micros,)),
-            dma((4,)),
+            dma((1,)),
+            dma((5,)),
         ],
         compiler_params=pltpu.CompilerParams(
             collective_id=0, has_side_effects=True, vmem_limit_bytes=58 * 1024 * 1024
@@ -497,10 +517,14 @@
         padded[:, :divide_position].reshape(block_total, owner_total, width * ADAPTER_RANK),
         (1, 0, 2),
     )
-    adapter_down = lax.psum_scatter(down_part, "dp", scatter_dimension=0, tiled=False)
-    adapter_up = lax.psum(padded[:, divide_position:], "dp").reshape(ranks, value_feature_width)
+    up_part = padded[:, divide_position:].reshape(owner_total, block_total, -1)
+    owned_parts = lax.psum_scatter(
+        jnp.concatenate([down_part, up_part], axis=2), "dp", scatter_dimension=0, tiled=False
+    )
+    adapter_up = owned_parts[:, width * ADAPTER_RANK :].reshape(-1, value_feature_width)
     adapter_down = jnp.transpose(
-        adapter_down.reshape(block_total, width, ADAPTER_RANK), (1, 0, 2)
+        owned_parts[:, : width * ADAPTER_RANK].reshape(block_total, width, ADAPTER_RANK),
+        (1, 0, 2),
     ).reshape(width, ranks)
     rows = owner_total * MROWS
     mask = (
@@ -556,11 +580,25 @@
     )
     slot_counts = jnp.where(live, slot_counts, 1)
     slot_grad = summed / slot_counts.astype(jnp.float32)[:, None]
+    slot_of_block = jnp.argmax(own_select, axis=1)
+    block_params, _, _ = adam_update(
+        slot_adapter_params[0][slot_of_block],
+        first_moment[0][slot_of_block],
+        second_moment[0][slot_of_block],
+        slot_grad[slot_of_block],
+        jnp.any(own_select, axis=1)[:, None],
+    )
+    returned = assemble(
+        lax.all_to_all(
+            block_params.reshape(owner_total, local_blocks, panel_width),
+            "dp",
+            split_axis=0,
+            concat_axis=0,
+            tiled=True,
+        )
+    )
     params_new, first_new, second_new = adam_update(
         slot_adapter_params[0], first_moment[0], second_moment[0], slot_grad, live[:, None]
-    )
-    returned = assemble(
-        lax.all_to_all(hand_out(params_new), "dp", split_axis=0, concat_axis=0, tiled=True)
     )
     return (params_new[None], first_new[None], second_new[None], returned[None])
 

time: 561 us -> 512 us (0.913)
  waiting for transfers between devices: 111 us -> 42.7 us
  other arithmetic: 30.5 us -> 50.1 us
  local copies, waits for them, and re-layouts: 23.5 us -> 42.5 us
  matrix products: 24.8 us -> 12.7 us
  Pallas kernels: 353 us -> 345 us
    psum x1 -> x0, waiting for transfers between devices: 52.4 us -> none  [on_device(): lax.psum(padded[:, divide_position:], 'dp')]
    gather x0 -> x4, local copies, waits for them, and re-layouts: none -> 21.6 us  [the longest x1 6.05 us: on_device(): slot_grad[slot_of_block]]
    all_gather x1, waiting for transfers between devices: 22.2 us -> 5.6 us  [on_device(): down_grads = lax.all_gather(down_grads, 'dp', axis=1, tiled=True)]
    broadcast_in_dim x1 -> x2, other arithmetic: 17.6 us -> 31.5 us  [on_device(): return (params_new[None], first_new[None], second_new[None], returned[None])]
    dot_general x3, matrix products: 20.9 us -> 9.56 us  [dot_tn(): lax.dot_general(left, right, (((0,), (0,)), ((), ())), preferred_element_...]
    pallas_call x1, Pallas kernels: 353 us -> 345 us  [run_layers(): pl.pallas_call(functools.partial(layers_kernel, dims), out_shape=(jax.Sha...]
  transfers between devices with their start and end apart: 4 -> 3, of which waited for: 3 -> 2; matrix products, arithmetic and copies ran while one was open for 5% -> 11% of each run, Pallas kernels for 0% -> 0%
where the time goes in v2:
time: 512 us; the launch traced here: 511 us
  Pallas kernels  345 us (67%)
  other arithmetic  50.1 us (10%)
  waiting for transfers between devices  42.7 us (8%)
  local copies, waits for them, and re-layouts  42.5 us (8%)
  between operations  14.4 us (3%)
  matrix products  12.7 us (2%)
    pallas_call x1, Pallas kernels, run_layers(): pl.pallas_call(functools.partial(layers_kernel, dims), out_shape=(jax.Sha...  345 us
    reduce_scatter x1, waiting for transfers between devices, on_device(): lax.psum_scatter(jnp.concatenate([down_part, up_part], axis=2), 'dp', sca...  37.1 us
    broadcast_in_dim x2, other arithmetic, on_device(): return (params_new[None], first_new[None], second_new[None], returned[None])  31.5 us
  transfers between devices with their start and end apart: 3, of which 2 were waited for; matrix products, arithmetic and copies ran while one was open for 11% of the time, Pallas kernels for 0%

profile of v2, /device:TPU:0, one launch (start us, length us, event | category | flops | bytes accessed | tf_op | source)
XLA Modules:
  0.0 510.8 jit_solution(8736240071246827041)
XLA Ops:
  7.2 0.7 compare_bitcast_fusion
  7.9 0.7 broadcast_compare_fusion.2
  8.6 0.7 fusion.33
  9.3 0.8 select_reduce_fusion.2
  10.2 3.1 convolution_convert_fusion
  13.3 0.3 broadcast_select_fusion
  13.9 1.6 pad_maximum_fusion
  15.6 0.6 constant_dynamic-slice_fusion.gain
  16.2 0.7 fusion.23.fold
  16.9 0.7 fusion.32
  17.6 37.1 %reduce-scatter.2.cloned.1.call-done = bf16[1,8,18432]{2,1,0:T(8,128)(2,1)} async-done(((bf16[8,8,18432]{2,1,0:T(8,128)(2,1)}), bf16[1,8,18432]{2,1,0:T(8,128)(2,1)}) %reduce-scatter.2.cloned.1.call-update) | async-done | bytes 294928 | tf_op jit(solution)/shard_map/reduce_scatter | solution.py:521
  54.7 0.8 slice.45
  55.5 1.0 slice.44
  56.4 0.6 reshape.322.bpart
  57.1 1.7 reshape.320
  58.8 0.8 copy.34
  59.6 0.8 copy.35.aw
  60.4 344.6 %shard_map.147 = (bf16[8,128,1024]{2,1,0:T(8,128)(2,1)}, bf16[8,128,1152]{2,1,0:T(8,128)(2,1)}, bf16[8,128,1024]{2,1,0:T(8,128)(2,1)}, bf16[8,128,128]{2,1,0:T(8,128)(2,1)}) custom-call(bf16[128,8192]{1,0:T(8,128)(2,1)} %tok.1, bf16[128,8192]{1,0:T(8,128)(2,1)} %cot.1, f32[1,1024]{1,0:T(1,128)} %constant_dynamic-slice_fusion.gain, ...), custom_call_target="tpu_custom_call" | custom-call | tf_op jit(solution)/shard_map/pallas_call | solution.py:408
  405.0 1.4 add_reduce_fusion
  406.5 2.4 fusion.9
  408.8 1.0 copy.37
  409.9 4.5 reshape.324
  414.5 0.6 dynamic_slice.16
  415.2 0.8 iota_reduce_fusion
  416.0 5.2 %gather_fusion = bf16[8,36864]{1,0:T(8,128)(2,1)} fusion(bf16[64,36864]{1,0:T(8,128)(2,1)} %bitcast.95, s32[1024]{0:T(1024)S(1)} %pad_clamp_fusion), kind=kCustom, calls=%fused_computation | custom fusion | bytes 1179680 | tf_op jit(solution)/shard_map/gather | solution.py:585
  421.2 5.1 %gather_fusion.3 = f32[8,36864]{1,0:T(8,128)S(1)} fusion(f32[64,36864]{1,0:T(8,128)} %bitcast.91, s32[1024]{0:T(1024)S(1)} %pad_clamp_fusion), kind=kCustom, calls=%fused_computation.3 | custom fusion | bytes 2359328 | tf_op jit(solution)/shard_map/gather | solution.py:587
  426.3 5.2 %gather_fusion.1 = f32[8,36864]{1,0:T(8,128)S(1)} fusion(f32[64,36864]{1,0:T(8,128)} %bitcast.94, s32[1024]{0:T(1024)S(1)} %pad_clamp_fusion), kind=kCustom, calls=%fused_computation.1 | custom fusion | bytes 2359328 | tf_op jit(solution)/shard_map/gather | solution.py:586
  431.6 0.7 broadcast_compare_fusion.1
  432.5 0.2 select_reduce_fusion
  432.6 0.2 fusion.25
  432.8 1.0 slice.31
  434.0 2.1 fusion.10
  436.2 5.6 %all-gather.2.cloned.1.call-done = bf16[8,131072]{1,0:T(8,128)(2,1)} async-done(((bf16[8,16384]{1,0:T(8,128)(2,1)}), bf16[8,131072]{1,0:T(8,128)(2,1)}) %all-gather.2.cloned.1.call-update) | async-done | bytes 2097168 | tf_op jit(solution)/shard_map/all_gather | solution.py:568
  441.8 5.6 %pad_maximum_fusion.1 = bf16[8,147456]{1,0:T(8,128)(2,1)S(1)} fusion(bf16[8,16384]{1,0:T(8,128)(2,1)S(1)} %reshape.325, bf16[8,131072]{1,0:T(8,128)(2,1)} %all-gather.2.cloned.1.call-done), kind=kLoop, calls=%fused_computation.19 | loop fusion | flops 4718592 | bytes 4718592 | tf_op jit(solution)/shard_map/concatenate | solution.py:569
  447.4 0.6 fusion.2
  448.0 5.1 %convolution_divide_fusion = f32[64,36864]{1,0:T(8,128)} fusion(f32[64]{0:T(128)S(1)} %select_convert_fusion, bf16[8,36864]{1,0:T(8,128)(2,1)S(1)} %fusion.2, s32[64]{0:T(128)S(1)} %get-tuple-element.15, s32[8]{0:T(128)S(1)} %copy-done.3, pred[64]{0:T(512)(128)(4,1)S(1)} %compare_bitcast_fusion), kind=kOutput, calls=%fused_computation.5 | convolution fusion | flops 40109056 | bytes 10027616 | tf_op jit(solution)/shard_map/dot_general | solution.py:33
  453.1 6.1 %gather_fusion.2 = f32[8,36864]{1,0:T(8,128)} fusion(f32[64,36864]{1,0:T(8,128)} %convolution_divide_fusion, s32[1024]{0:T(1024)S(1)} %pad_clamp_fusion), kind=kCustom, calls=%fused_computation.2 | custom fusion | bytes 2359328 | tf_op jit(solution)/shard_map/gather | solution.py:588
  459.2 2.3 fusion.21
  461.5 0.5 broadcast.333
  462.0 1.1 reduce.22
  463.1 1.3 reshape.375
  464.3 3.8 all-to-all-start
  468.1 17.9 %select_bitcast_fusion = (f32[1,64,36864]{2,1,0:T(8,128)}, f32[1,64,36864]{2,1,0:T(8,128)}) fusion(f32[64,36864]{1,0:T(8,128)} %convolution_divide_fusion, pred[64]{0:T(512)(128)(4,1)S(1)} %get-tuple-element.14, f32[1,64,36864]{2,1,0:T(8,128)} %param.23, f32[1,64,36864]{2,1,0:T(8,128)} %param.22), kind=kLoop, calls=%fused_computation.9 | loop fusion | flops 21233664 | bytes 47185984 | tf_op jit(solution)/shard_map/broadcast_in_dim | solution.py:603
  486.0 13.6 %fusion.3 = bf16[1,64,36864]{2,1,0:T(8,128)(2,1)} fusion(f32[64,36864]{1,0:T(8,128)} %convolution_divide_fusion, pred[64]{0:T(512)(128)(4,1)S(1)} %get-tuple-element.14, f32[1,64,36864]{2,1,0:T(8,128)S(1)} %bitcast.93, f32[1,64,36864]{2,1,0:T(8,128)} %param.22, bf16[1,64,36864]{2,1,0:T(8,128)(2,1)} %param.21), kind=kLoop, calls=%fused_computation.16 | loop fusion | flops 37748736 | bytes 37748800 | tf_op jit(solution)/shard_map/broadcast_in_dim | solution.py:603
  499.7 0.6 reshape.376
  500.3 0.7 copy.41
  500.9 1.9 gather_fusion.4
  502.8 1.2 broadcast_in_dim_reshape.3
  (43 shorter events, 1.1 us)
Async XLA Ops:
  7.2 8.4 %copy-start = (f32[1,8192]{1,0:T(1,128)S(1)}, f32[1,8192]{1,0:T(1,128)}, u32[]{:S(2)}) copy-start(f32[1,8192]{1,0:T(1,128)} %param.14) | copy-start | bytes 98308
  7.2 47.5 %reduce-scatter.2.cloned.1.call-start = ((), (), s32[]{:S(2)}) async-start(), calls=%async_computation.2 | async-start | bytes 2654208 | tf_op jit(solution)/shard_map/reduce_scatter | solution.py:521
  15.5 426.3 %all-gather.2.cloned.1.call-start = ((), (), s32[]{:S(2)}) async-start(), calls=%async_computation.3 | async-start | bytes 2359296 | tf_op jit(solution)/shard_map/all_gather | solution.py:568
  60.4 346.0 %copy-start.2 = (f32[1,1024]{1,0:T(1,128)S(1)}, f32[1,1024]{1,0:T(1,128)}, u32[]{:S(2)}) copy-start(f32[1,1024]{1,0:T(1,128)} %constant_dynamic-slice_fusion.gain) | copy-start | bytes 12292
  408.8 5.6 %copy-start.3 = (s32[8]{0:T(128)S(1)}, s32[8]{0:T(128)}, u32[]{:S(2)}) copy-start(s32[8]{0:T(128)} %param.17) | copy-start | bytes 100
  426.3 5.3 %copy-start.4 = (s32[8,64]{1,0:T(8,128)S(1)}, s32[8,64]{1,0:T(8,128)}, u32[]{:S(2)}) copy-start(s32[8,64]{1,0:T(8,128)} %param.18) | copy-start | bytes 6148
  426.3 5.9 %copy-start.5 = (s32[8,64]{1,0:T(8,128)S(1)}, s32[8,64]{1,0:T(8,128)}, u32[]{:S(2)}) copy-start(s32[8,64]{1,0:T(8,128)} %param.19) | copy-start | bytes 6148
  426.3 6.1 %copy-start.6 = (s32[64]{0:T(128)S(1)}, s32[64]{0:T(128)}, u32[]{:S(2)}) copy-start(s32[64]{0:T(128)} %param.20) | copy-start | bytes 772
  463.1 22.9 %slice-start = ((s8[9437184]{0:T(1024)(128)(4,1)}), s8[1048576]{0:T(1024)(128)(4,1)S(1)}, s32[]{:S(2)}) async-start(s8[9437184]{0:T(1024)(128)(4,1)} %bitcast.92), calls=%async_computation.4 | async-start | bytes 2097152
  464.3 35.3 %all-to-all-start = ((bf16[8,2,18432]{2,1,0:T(2,128)(2,1)}), bf16[8,2,18432]{2,1,0:T(2,128)(2,1)S(1)}, u32[]{:S(2)}, u32[]{:S(2)}) async-start(bf16[8,2,18432]{2,1,0:T(2,128)(2,1)} %reshape.375), calls=%async_computation.1 | async-start | bytes 1179648 | tf_op jit(solution)/shard_map/all_to_all | solution.py:592
  468.1 17.9 %slice-start.1 = ((s8[9437184]{0:T(1024)(128)(4,1)}), s8[4194304]{0:T(1024)(128)(4,1)S(1)}, s32[]{:S(2)}) async-start(s8[9437184]{0:T(1024)(128)(4,1)} %bitcast.92), calls=%async_computation.5 | async-start | bytes 8388608
  468.1 17.9 %slice-start.2 = ((s8[9437184]{0:T(1024)(128)(4,1)}), s8[4194304]{0:T(1024)(128)(4,1)S(1)}, s32[]{:S(2)}) async-start(s8[9437184]{0:T(1024)(128)(4,1)} %bitcast.92), calls=%async_computation.6 | async-start | bytes 8388608
  499.7 4.3 copy-start.1
Sparse Core Ops, SparseCore 0:
  15.6 39.0 reduce-scatter.1
  414.6 27.1 all-gather.1

commit v3 on v2

--- a/solution.py
+++ b/solution.py
@@ -48,12 +48,17 @@
     bpart,
     mask,
     fold,
+    vt,
+    ot,
+    at,
+    unfold,
     h,
     val,
     gv,
     gl,
     dh,
     bw,
+    bt,
     snd_f,
     pr_f,
     mid_f,
@@ -240,7 +245,7 @@
     back = Reduce(snd_b, pr_b, mid_b, rs_b, gv, sem_b, plain, plain)
 
     def wide_low(tail):
-        spread_low = dot_nt(tail, fold[...])
+        spread_low = dot_nn(tail, unfold[...])
         return jnp.where(mask[...] > 0, spread_low, 0.0).astype(BF)
 
     def ahead_start(m):
@@ -269,7 +274,7 @@
             value = (
                 val[m, :, :features].astype(F32) + ADAPTER_SCALE * dot_nn(low, bw[...])
             ).astype(BF)
-            result = (h[m].astype(F32) + dot_nt(value, ow[...])).astype(BF)
+            result = (h[m].astype(F32) + dot_nn(value, ot[...])).astype(BF)
 
             @pl.when(m > 0)
             def _():
@@ -298,7 +303,7 @@
         back.arrive(m)
         grad_value = gv[m]
         grad_low = jnp.where(
-            mask[...] > 0, ADAPTER_SCALE * dot_nt(grad_value, bw[...]), 0.0
+            mask[...] > 0, ADAPTER_SCALE * dot_nn(grad_value, bt[...]), 0.0
         ).astype(BF)
         gl[m] = grad_low
 
@@ -310,7 +315,7 @@
             inner = jnp.sum(
                 grad_value.astype(F32) * val[m, :, :features].astype(F32), axis=1, keepdims=True
             ) + jnp.sum(grad_low.astype(F32) * low.astype(F32), axis=1, keepdims=True)
-            norm_grad = (dot_nt(grad_value, vw[...]) + dot_nt(grad_low, aw[...])) * gain[...]
+            norm_grad = (dot_nn(grad_value, vt[...]) + dot_nn(grad_low, at[...])) * gain[...]
             result = (
                 dh[m].astype(F32)
                 + scale * norm_grad
@@ -346,6 +351,7 @@
     bw[up_place, :] = bpart[...]
     others = bw.at[pl.ds(0, (n - 1) * part_rows)]
     wait_bytes(others, up_sem.at[0])
+    bt[...] = bw[...].astype(F32).T.astype(BF)
 
     def step(t, carry):
         m_f = t - s
@@ -394,7 +400,7 @@
         wait_bytes(cot.at[:, pl.ds(0, (n - 1) * width)], send_sem.at[3])
 
 
-def run_layers(tokens, cotangent, gain, vw, ow, aw, bw, mask, fold):
+def run_layers(tokens, cotangent, gain, vw, ow, aw, bw, mask, fold, at):
     sections, n = lax.axis_size("section"), lax.axis_size("dp")
     q = MROWS
     width, features = vw.shape
@@ -413,11 +419,12 @@
             jax.ShapeDtypeStruct((micros, rows, features), BF),
             jax.ShapeDtypeStruct((micros, rows, ranks), BF),
         ),
-        in_specs=[vmem] * 9,
+        in_specs=[vmem] * 13,
         out_specs=(vmem,) * 4,
         scratch_shapes=[
             pltpu.VMEM((micros, rows, width), BF),
             pltpu.VMEM((ranks, features), BF),
+            pltpu.VMEM((features, ranks), BF),
             pltpu.VMEM((rows, wide), BF),
             pltpu.VMEM((rows // 2, wide), BF),
             pltpu.VMEM((rows // 2, wide), BF),
@@ -440,7 +447,56 @@
         compiler_params=pltpu.CompilerParams(
             collective_id=0, has_side_effects=True, vmem_limit_bytes=58 * 1024 * 1024
         ),
-    )(tokens, cotangent, gain, vw, ow, aw, bw, mask, fold)
+    )(tokens, cotangent, gain, vw, ow, aw, bw, mask, fold, vw.T, ow.T, at, fold.T)
+
+
+def adam_kernel(own, counts, live, arrived, params, first, second, params_out, first_out, second_out):
+    slot_grad = dot_nn(own[...], arrived[...]) / counts[...]
+    on = live[...] > 0
+    first_old, second_old = first[...], second[...]
+    params_old = params[...].astype(F32)
+    first_step = BETA_FIRST * first_old + (1.0 - BETA_FIRST) * slot_grad
+    second_step = BETA_SECOND * second_old + (1.0 - BETA_SECOND) * slot_grad * slot_grad
+    step_size = first_step / FIRST_FIX / (jnp.sqrt(second_step / SECOND_FIX) + ADAM_EPS)
+    params_out[...] = jnp.where(on, params_old - LEARN_RATE * step_size, params_old).astype(BF)
+    first_out[...] = jnp.where(on, first_step, first_old)
+    second_out[...] = jnp.where(on, second_step, second_old)
+
+
+def run_adam(own, counts, live, arrived, params, first, second):
+    slots, panel = params.shape
+    blocks = arrived.shape[0]
+    tile = max(k for k in range(128, 4609, 128) if panel % k == 0)
+
+    def whole(*shape):
+        return pl.BlockSpec(shape, lambda i: (0, 0))
+
+    def cut(count):
+        return pl.BlockSpec((count, tile), lambda i: (0, i))
+
+    return pl.pallas_call(
+        adam_kernel,
+        grid=(panel // tile,),
+        out_shape=(
+            jax.ShapeDtypeStruct((slots, panel), BF),
+            jax.ShapeDtypeStruct((slots, panel), F32),
+            jax.ShapeDtypeStruct((slots, panel), F32),
+        ),
+        in_specs=[
+            whole(slots, blocks),
+            whole(slots, 1),
+            whole(slots, 1),
+            cut(blocks),
+            cut(slots),
+            cut(slots),
+            cut(slots),
+        ],
+        out_specs=(cut(slots),) * 3,
+        compiler_params=pltpu.CompilerParams(vmem_limit_bytes=48 * 1024 * 1024),
+        cost_estimate=pl.CostEstimate(
+            flops=20 * slots * panel, bytes_accessed=20 * slots * panel, transcendentals=0
+        ),
+    )(own, counts, live, arrived, params, first, second)
 
 
 def adam_update(params_old, first_old, second_old, slot_grad, live):
@@ -522,10 +578,11 @@
         jnp.concatenate([down_part, up_part], axis=2), "dp", scatter_dimension=0, tiled=False
     )
     adapter_up = owned_parts[:, width * ADAPTER_RANK :].reshape(-1, value_feature_width)
-    adapter_down = jnp.transpose(
+    down_turned = jnp.transpose(
         owned_parts[:, : width * ADAPTER_RANK].reshape(block_total, width, ADAPTER_RANK),
-        (1, 0, 2),
-    ).reshape(width, ranks)
+        (0, 2, 1),
+    ).reshape(ranks, width)
+    adapter_down = down_turned.T
     rows = owner_total * MROWS
     mask = (
         jnp.arange(rows, dtype=jnp.int32)[:, None] // MROWS
@@ -545,6 +602,7 @@
         adapter_up,
         mask.astype(F32),
         fold,
+        down_turned,
     )
     total_rows = hidden.shape[0] * rows
     tail = val[:, :, value_feature_width:]
@@ -569,23 +627,21 @@
     block_grads = jnp.concatenate(
         [down_grads, up_grads.reshape(block_total, ADAPTER_RANK * value_feature_width)], axis=1
     ).reshape(block_total, slab_count, panel_width)
-    arrived = jnp.sum(
-        jnp.where(held[:, :, None], block_grads.astype(F32), 0.0), axis=1
-    ).astype(BF)
-    summed = dot_tn(own_select.astype(BF), arrived)
+    arrived = jnp.sum(jnp.where(held[:, :, None], block_grads.astype(F32), 0.0), axis=1)
+    same = (block_adapter_ids[:, None] == block_adapter_ids[None, :]).astype(F32)
+    block_grad = dot_nn(same, arrived) / token_counts[block_adapter_ids].astype(F32)[:, None]
     live = my_jobs >= 0
     adapter_ids = jnp.arange(adapter_total, dtype=jnp.int32)
     slot_counts = jnp.sum(
         jnp.where(adapter_ids[None, :] == my_jobs[:, None], token_counts[None, :], 0), axis=1
     )
     slot_counts = jnp.where(live, slot_counts, 1)
-    slot_grad = summed / slot_counts.astype(jnp.float32)[:, None]
     slot_of_block = jnp.argmax(own_select, axis=1)
     block_params, _, _ = adam_update(
         slot_adapter_params[0][slot_of_block],
         first_moment[0][slot_of_block],
         second_moment[0][slot_of_block],
-        slot_grad[slot_of_block],
+        block_grad,
         jnp.any(own_select, axis=1)[:, None],
     )
     returned = assemble(
@@ -597,8 +653,14 @@
             tiled=True,
         )
     )
-    params_new, first_new, second_new = adam_update(
-        slot_adapter_params[0], first_moment[0], second_moment[0], slot_grad, live[:, None]
+    params_new, first_new, second_new = run_adam(
+        own_select.astype(F32).T,
+        slot_counts.astype(F32)[:, None],
+        live.astype(F32)[:, None],
+        arrived,
+        slot_adapter_params[0],
+        first_moment[0],
+        second_moment[0],
     )
     return (params_new[None], first_new[None], second_new[None], returned[None])
 

time: 512 us -> 491 us (0.959)
  other arithmetic: 50.1 us -> 16.6 us
  Pallas kernels: 345 us -> 362 us
  waiting for transfers between devices: 42.7 us -> 31.8 us
  local copies, waits for them, and re-layouts: 42.5 us -> 52.8 us
    broadcast_in_dim x2 -> x0, other arithmetic: 31.5 us -> none  [on_device(): return (params_new[None], first_new[None], second_new[None], returned[None])]
    pallas_call x0 -> x1, Pallas kernels: none -> 20 us  [run_adam(): pl.pallas_call(adam_kernel, grid=(panel // tile,), out_shape=(jax.ShapeDt...]
    unnamed x23 -> x31, local copies, waits for them, and re-layouts: 2.06 us -> 13.2 us
    reduce_scatter x1, waiting for transfers between devices: 37.1 us -> 29.2 us  [on_device(): lax.psum_scatter(jnp.concatenate([down_part, up_part], axis=2), 'dp', sca...]
    dot_general x3 -> x2, matrix products: 9.56 us -> 3.53 us  [dot_tn(): lax.dot_general(left, right, (((0,), (0,)), ((), ())), preferred_element_...]
    gather x1, local copies, waits for them, and re-layouts: 6.05 us -> 0.64 us  [on_device(): token_counts[block_adapter_ids].astype(F32)[:, None]]
  transfers between devices with their start and end apart: 3 -> 3, of which waited for: 2 -> 2; matrix products, arithmetic and copies ran while one was open for 11% -> 7% of each run, Pallas kernels for 0% -> 4%
where the time goes in v3:
time: 491 us; the launch traced here: 489 us
  Pallas kernels  362 us (74%)
  local copies, waits for them, and re-layouts  52.8 us (11%)
  waiting for transfers between devices  31.8 us (6%)
  other arithmetic  16.6 us (3%)
  between operations  14.4 us (3%)
  matrix products  8.67 us (2%)
    pallas_call x1, Pallas kernels, run_layers(): pl.pallas_call(functools.partial(layers_kernel, dims), out_shape=(jax.Sha...  342 us
    reduce_scatter x1, waiting for transfers between devices, on_device(): lax.psum_scatter(jnp.concatenate([down_part, up_part], axis=2), 'dp', sca...  29.2 us
    pallas_call x1, Pallas kernels, run_adam(): pl.pallas_call(adam_kernel, grid=(panel // tile,), out_shape=(jax.ShapeDt...  20 us
    unnamed x31, local copies, waits for them, and re-layouts  13.2 us
  transfers between devices with their start and end apart: 3, of which 2 were waited for; matrix products, arithmetic and copies ran while one was open for 7% of the time, Pallas kernels for 4%

profile of v3, /device:TPU:0, one launch (start us, length us, event | category | flops | bytes accessed | tf_op | source)
XLA Modules:
  0.0 489.5 jit_solution(17027095951764779143)
XLA Ops:
  7.2 0.7 fusion.31
  7.9 0.7 fusion.32
  8.6 0.7 fusion.29
  9.3 0.8 select_reduce_fusion.2
  10.2 3.1 convolution_convert_fusion
  13.9 1.6 pad_maximum_fusion
  15.5 1.5 copy-done.4
  17.1 2.5 copy.73
  19.6 3.9 copy.74
  23.5 0.6 constant_dynamic-slice_fusion.gain
  24.1 0.7 fusion.19
  24.8 0.7 fusion.28
  25.5 29.2 %reduce-scatter.2.cloned.1.call-done = bf16[1,8,18432]{2,1,0:T(8,128)(2,1)} async-done(((bf16[8,8,18432]{2,1,0:T(8,128)(2,1)}), bf16[1,8,18432]{2,1,0:T(8,128)(2,1)}) %reduce-scatter.2.cloned.1.call-update) | async-done | bytes 294928 | tf_op jit(solution)/shard_map/reduce_scatter | solution.py:577
  54.7 0.8 slice.45
  55.5 1.0 slice.44
  56.4 0.6 reshape.257.bpart
  57.0 1.7 reshape.255
  58.8 0.8 copy.75
  59.5 0.8 copy.78.aw
  60.4 341.6 %shard_map.147 = (bf16[8,128,1024]{2,1,0:T(8,128)(2,1)}, bf16[8,128,1152]{2,1,0:T(8,128)(2,1)}, bf16[8,128,1024]{2,1,0:T(8,128)(2,1)}, bf16[8,128,128]{2,1,0:T(8,128)(2,1)}) custom-call(bf16[128,8192]{1,0:T(8,128)(2,1)} %tok.1, bf16[128,8192]{1,0:T(8,128)(2,1)} %cot.1, f32[1,1024]{1,0:T(1,128)} %constant_dynamic-slice_fusion.gain, ...), custom_call_target="tpu_custom_call" | custom-call | tf_op jit(solution)/shard_map/pallas_call | solution.py:414
  402.0 1.4 add_reduce_fusion
  403.4 2.4 fusion.6
  405.8 1.0 copy.80
  406.8 4.5 reshape.259
  412.0 0.7 iota_reduce_fusion
  412.7 0.6 gather_fusion.2
  413.5 5.2 %gather_fusion = bf16[8,36864]{1,0:T(8,128)(2,1)} fusion(bf16[64,36864]{1,0:T(8,128)(2,1)} %bitcast.69, s32[1024]{0:T(1024)S(1)} %pad_clamp_fusion.1), kind=kCustom, calls=%fused_computation | custom fusion | bytes 1179680 | tf_op jit(solution)/shard_map/gather | solution.py:641
  418.7 5.1 %gather_fusion.3 = f32[8,36864]{1,0:T(8,128)S(1)} fusion(f32[64,36864]{1,0:T(8,128)} %bitcast.73, s32[1024]{0:T(1024)S(1)} %pad_clamp_fusion.1), kind=kCustom, calls=%fused_computation.3 | custom fusion | bytes 2359328 | tf_op jit(solution)/shard_map/gather | solution.py:643
  423.9 6.3 %gather_fusion.1 = f32[8,36864]{1,0:T(8,128)} fusion(f32[64,36864]{1,0:T(8,128)} %bitcast.71, s32[1024]{0:T(1024)S(1)} %pad_clamp_fusion.1), kind=kCustom, calls=%fused_computation.1 | custom fusion | bytes 2359328 | tf_op jit(solution)/shard_map/gather | solution.py:642
  430.5 0.7 broadcast_compare_fusion.1
  431.2 1.7 slice.31
  432.9 1.1 copy.82
  434.0 1.2 fusion.7
  435.1 1.1 reshape.260
  436.2 2.6 all-gather.2.cloned.1.call-done
  438.8 5.6 %pad_maximum_fusion.1 = bf16[8,147456]{1,0:T(8,128)(2,1)S(1)} fusion(bf16[8,16384]{1,0:T(8,128)(2,1)S(1)} %reshape.260, bf16[8,131072]{1,0:T(8,128)(2,1)} %all-gather.2.cloned.1.call-done), kind=kLoop, calls=%fused_computation.11 | loop fusion | flops 4718592 | bytes 4718592 | tf_op jit(solution)/shard_map/concatenate | solution.py:627
  444.5 0.6 fusion.arrived
  445.1 0.6 copy-done.7
  445.9 2.0 fusion.17
  448.4 2.1 reduce.22
  450.6 1.3 reshape.311
  451.8 3.5 all-to-all-start
  456.0 2.3 copy-done.2
  458.3 20.0 %shard_map.148 = (bf16[64,36864]{1,0:T(8,128)(2,1)}, f32[64,36864]{1,0:T(8,128)}, f32[64,36864]{1,0:T(8,128)}) custom-call(f32[64,8]{1,0:T(8,128)S(1)} %and_convert_fusion.own, f32[64,1]{1,0:T(8,128)S(1)} %select_convert_fusion.counts, f32[64,1]{1,0:T(8,128)S(1)} %copy.83.live, f32[8,36864]{1,0:T(8,128)S(1)} %fusion.arrived, bf16[64,36864]{1,0:T(8,128)(2,1)S(1)} %bitcast.70, ...), custom_call_target="tpu_custom_call" | custom-call | flops 47185920 | bytes 47185920 | tf_op jit(solution)/shard_map/pallas_call | solution.py:477
  478.3 0.6 reshape.312
  478.9 0.7 copy.85
  479.6 1.9 gather_fusion.4
  481.5 1.2 broadcast_in_dim_reshape.3
  (53 shorter events, 3.1 us)
Async XLA Ops:
  7.2 16.4 %copy-start = (f32[1,8192]{1,0:T(1,128)S(1)}, f32[1,8192]{1,0:T(1,128)}, u32[]{:S(2)}) copy-start(f32[1,8192]{1,0:T(1,128)} %param.14) | copy-start | bytes 98308
  7.2 47.5 %reduce-scatter.2.cloned.1.call-start = ((), (), s32[]{:S(2)}) async-start(), calls=%async_computation.2 | async-start | bytes 2654208 | tf_op jit(solution)/shard_map/reduce_scatter | solution.py:577
  15.5 1.6 copy-start.4
  15.5 423.3 %all-gather.2.cloned.1.call-start = ((), (), s32[]{:S(2)}) async-start(), calls=%async_computation.3 | async-start | bytes 2359296 | tf_op jit(solution)/shard_map/all_gather | solution.py:626
  59.5 0.9 copy-start.5
  60.4 343.0 %copy-start.10 = (f32[1,1024]{1,0:T(1,128)S(1)}, f32[1,1024]{1,0:T(1,128)}, u32[]{:S(2)}) copy-start(f32[1,1024]{1,0:T(1,128)} %constant_dynamic-slice_fusion.gain) | copy-start | bytes 12292
  405.8 5.6 %copy-start.9 = (s32[8]{0:T(128)S(1)}, s32[8]{0:T(128)}, u32[]{:S(2)}) copy-start(s32[8]{0:T(128)} %param.17) | copy-start | bytes 100
  405.8 6.9 %copy-start.3 = (s32[64]{0:T(128)S(1)}, s32[64]{0:T(128)}, u32[]{:S(2)}) copy-start(s32[64]{0:T(128)} %param.20) | copy-start | bytes 772
  423.8 6.7 %copy-start.11 = (s32[8,64]{1,0:T(8,128)S(1)}, s32[8,64]{1,0:T(8,128)}, u32[]{:S(2)}) copy-start(s32[8,64]{1,0:T(8,128)} %param.18) | copy-start | bytes 6148
  423.8 10.1 %copy-start.6 = (bf16[8,128,1024]{2,1,0:T(8,128)(2,1)S(1)}, bf16[8,128,1024]{2,1,0:T(8,128)(2,1)}, u32[]{:S(2)}) copy-start(bf16[8,128,1024]{2,1,0:T(8,128)(2,1)} %get-tuple-element.15) | copy-start | bytes 6291460
  444.5 1.3 copy-start.7
  444.5 1.4 copy-start.8
  447.9 7.5 %copy-start.12 = (s32[8,64]{1,0:T(8,128)S(1)}, s32[8,64]{1,0:T(8,128)}, u32[]{:S(2)}) copy-start(s32[8,64]{1,0:T(8,128)} %param.19) | copy-start | bytes 6148
  451.8 26.5 %all-to-all-start = ((bf16[8,2,18432]{2,1,0:T(2,128)(2,1)}), bf16[8,2,18432]{2,1,0:T(2,128)(2,1)S(1)}, u32[]{:S(2)}, u32[]{:S(2)}) async-start(bf16[8,2,18432]{2,1,0:T(2,128)(2,1)} %reshape.311), calls=%async_computation.1 | async-start | bytes 1179648 | tf_op jit(solution)/shard_map/all_to_all | solution.py:648
  456.0 2.3 copy-start.2
  478.9 3.7 copy-start.1
Sparse Core Ops, SparseCore 0:
  15.6 39.0 reduce-scatter.1
  411.5 27.2 all-gather.1
